TPU v7x, 32 devices: a whole 2x2x4 slice. The times are simulated.
32 devices in a mesh: sky: 2 (over x), seg: 16 (over z, y, core).
Axes of the slice: x: 2, y: 2, z: 4, core: 2. Of those that a mesh axis runs over, the one named last changes fastest.
Arguments:
- strain_series: bfloat16 [32, 2, 65536], P(('sky', 'seg')), parts along dimension 0, may hold values from -6 to 6
- antenna: float32 [32, 2, 65536], P(('sky', 'seg')), parts along dimension 0, may hold values from -160 to 160, as said below
- drift: int32 [32, 6], P(('sky', 'seg')), parts along dimension 0, may hold values from -2 to 2
- tracks: int32 [64, 16], replicated, may hold values from 0 to 5
Outputs:
- track_stat: float32 [128, 65536], P('sky', 'seg'), parts along dimension 0
There are 2 independent parts, one for each index of `sky`. A program takes and returns all parts, laid end to end along the dimension named above; an argument that names none is the same for every part. Nothing has to cross between parts.
Inputs may be any that keep to these rules, and one draw needn't show every extreme that they name: `antenna`: row 0 holds the a weights, row 1 the b weights of each segment.
All inputs are finite; a program needn't handle non-finite values.
Results may differ from a plain program's by a relative error of at most 0.0015.
Values sent between devices are 32-bit elements; how exact they have to be, the bound alone decides.
No kernel may reach another device: no remote copies, remote signals or barrier semaphores. Data moves between devices by JAX's collectives and lax.ppermute only.
A program may use at most 192 MiB of HBM per device.

v0:
```python
import math

import jax
import jax.numpy as jnp
from jax import lax
from jax.sharding import PartitionSpec as P

DFT_ROWS = 256
BLK = 128
DMAX = 2
KCOH = 6


chirp_step = 3.0
tiny_eps = 1e-06


def section_tables(points, first_rows):
    second_rows = points // first_rows
    outer_index = jnp.arange(first_rows, dtype=jnp.int32)
    inner_index = jnp.arange(second_rows, dtype=jnp.int32)
    first_angle = (
        2.0
        * math.pi
        / first_rows
        * (outer_index[:, None] * outer_index[None, :] % first_rows).astype(jnp.float32)
    )
    cos_one, sin_one = (jnp.cos(first_angle), jnp.sin(first_angle))
    left_table = jnp.stack([jnp.stack([cos_one, sin_one]), jnp.stack([-sin_one, cos_one])]).astype(
        jnp.bfloat16
    )
    second_angle = (
        2.0
        * math.pi
        / second_rows
        * (inner_index[:, None] * inner_index[None, :] % second_rows).astype(jnp.float32)
    )
    cos_two, sin_two = (jnp.cos(second_angle), jnp.sin(second_angle))
    right_table = jnp.stack([jnp.stack([cos_two, -sin_two]), jnp.stack([sin_two, cos_two])]).astype(
        jnp.bfloat16
    )
    twist_angle = (
        2.0
        * math.pi
        / points
        * (outer_index[:, None] * inner_index[None, :] % points).astype(jnp.float32)
    )
    return (left_table, right_table, jnp.cos(twist_angle), jnp.sin(twist_angle))


def coherent_stat(series, weights):
    seg_rows = series.shape[0]
    points = series.shape[2]
    left_table, right_table, twist_cos, twist_sin = section_tables(points, DFT_ROWS)
    second_rows = points // DFT_ROWS
    position = jnp.arange(points, dtype=jnp.float32) / points
    chirp_rate = (jnp.arange(KCOH, dtype=jnp.float32) - (KCOH - 1) / 2.0) * chirp_step
    phases = 2.0 * math.pi * chirp_rate[:, None] * (position * position)[None, :]
    phase_cos, phase_sin = (jnp.cos(phases), jnp.sin(phases))
    series_real = series[:, 0].astype(jnp.float32)[:, None, :]
    series_imag = series[:, 1].astype(jnp.float32)[:, None, :]
    demod_real = series_real * phase_cos + series_imag * phase_sin
    demod_imag = series_imag * phase_cos - series_real * phase_sin
    weight_a = weights[:, 0][:, None, :]
    weight_b = weights[:, 1][:, None, :]
    with_a = jnp.stack([weight_a * demod_real, weight_a * demod_imag], 2)
    with_b = jnp.stack([weight_b * demod_real, weight_b * demod_imag], 2)
    weighted = jnp.stack([with_a, with_b], 2).astype(jnp.bfloat16)
    weighted = weighted.reshape(seg_rows * KCOH * 2, 2, DFT_ROWS, second_rows)
    section_one = jnp.einsum(
        "oikn,binm->bokm", left_table, weighted, preferred_element_type=jnp.float32
    )
    one_real, one_imag = (section_one[:, 0], section_one[:, 1])
    twisted_real = one_real * twist_cos + one_imag * twist_sin
    twisted_imag = one_imag * twist_cos - one_real * twist_sin
    middle = jnp.stack([twisted_real, twisted_imag], 1).astype(jnp.bfloat16)
    spectra = jnp.einsum("bikm,ioml->bolk", middle, right_table, preferred_element_type=jnp.float32)
    spectra = spectra.reshape(seg_rows, KCOH, 2, 2, points)
    a_real, a_imag = (spectra[:, :, 0, 0], spectra[:, :, 0, 1])
    b_real, b_imag = (spectra[:, :, 1, 0], spectra[:, :, 1, 1])
    weight_aa = jnp.mean(weights[:, 0] * weights[:, 0], axis=-1) + tiny_eps
    weight_bb = jnp.mean(weights[:, 1] * weights[:, 1], axis=-1) + tiny_eps
    weight_ab = jnp.mean(weights[:, 0] * weights[:, 1], axis=-1)
    determinant = jnp.maximum(
        weight_aa * weight_bb - weight_ab * weight_ab, 0.1 * weight_aa * weight_bb
    )
    energy = (
        weight_bb[:, None, None] * (a_real * a_real + a_imag * a_imag)
        + weight_aa[:, None, None] * (b_real * b_real + b_imag * b_imag)
        - 2.0 * weight_ab[:, None, None] * (a_real * b_real + a_imag * b_imag)
    )
    return energy / (points * determinant[:, None, None])


def drift_blocks(padded, offsets, extent, amount):
    summed = jnp.zeros(padded.shape[:-2] + (amount, padded.shape[-1]), padded.dtype)
    for offset in range(-extent, extent + 1):
        window = padded[..., extent - offset : extent - offset + amount, :]
        summed = summed + jnp.where((offsets == offset)[..., None, None], window, 0.0)
    return summed


def shift_local(stats, drift):
    seg_rows = stats.shape[0]
    points = stats.shape[2]
    blocks = stats.reshape(seg_rows, KCOH, points // BLK, BLK)
    padded = jnp.pad(blocks, ((0, 0), (0, 0), (DMAX, DMAX), (0, 0)))
    return drift_blocks(padded, drift, DMAX, points // BLK).reshape(seg_rows, KCOH, points)


def track_combine(tracks, moved):
    levels = jnp.arange(KCOH, dtype=jnp.int32)
    pick = (tracks[:, :, None] == levels[None, None, :]).astype(jnp.float32)
    return jnp.einsum("jsk,skf->jf", pick, moved, precision=lax.Precision.HIGHEST)


def local(strain_series, antenna, drift, tracks):
    stats = coherent_stat(strain_series, antenna)
    seg_rows = stats.shape[0]
    segments = tracks.shape[1]
    shifted = shift_local(stats, drift)
    start = lax.axis_index("seg") * seg_rows
    mine = lax.dynamic_slice_in_dim(tracks, start, seg_rows, 1)
    partial_sum = track_combine(mine, shifted)
    result = lax.psum_scatter(partial_sum, "seg", scatter_dimension=1, tiled=True) / segments
    return result


def solution(mesh):
    return jax.shard_map(
        local,
        mesh=mesh,
        in_specs=(
            P(("sky", "seg"), None, None),
            P(("sky", "seg"), None, None),
            P(("sky", "seg"), None),
            P(),
        ),
        out_specs=P("sky", "seg"),
        check_vma=False,
    )
```

profile of v0, /device:TPU:16, one launch (start us, length us, event | category | flops | bytes accessed | tf_op | source)
XLA Modules:
  0.0 316.1 jit_solution(17125670687759056328)
XLA Ops:
  6.5 0.0 copy-start
  6.5 0.0 reduce-scatter.2.cloned.1.call-start
  6.6 1.0 fusion.35
  7.5 0.1 multiply_multiply_fusion
  7.6 1.8 negate_convert_fusion
  9.4 1.7 fusion.32
  11.1 1.2 compare_bitcast_fusion.4
  12.4 1.5 slice_convert_fusion
  13.8 0.0 copy-done.2
  13.8 1.9 multiply_reduce_fusion
  19.1 49.6 %multiply_convert_fusion.3 = (bf16[1,6,1,65536]{3,2,1,0:T(2,128)(2,1)S(1)}, bf16[1,6,1,65536]{3,2,1,0:T(2,128)(2,1)S(1)}, bf16[1,6,1,65536]{3,2,1,0:T(2,128)(2,1)S(1)}, bf16[1,6,1,65536]{3,2,1,0:T(2,128)(2,1)S(1)}) fusion(f32[65536]{0:T(1024)S(1)} %bitcast.78, f32[65536]{0:T(1024)S(1)} %bitcast.80, f32[65536]{0:T(1024)S(1)} %multiply_multiply_fusion, ...), kind=kLoop, calls=%fused_computation.26 | loop fusion | flops 5898240 | bytes 4456472 | tf_op jit(solution)/shard_map/convert.18
  68.8 6.7 %maximum_bitcast_fusion.4 = (bf16[1,6,1,2,65536]{4,3,2,1,0:T(2,128)(2,1)S(1)}, bf16[1,6,1,2,65536]{4,3,2,1,0:T(2,128)(2,1)S(1)}) fusion(bf16[1,6,1,65536]{3,2,1,0:T(2,128)(2,1)S(1)} %get-tuple-element.11, bf16[1,6,1,65536]{3,2,1,0:T(2,128)(2,1)S(1)} %get-tuple-element.10, bf16[1,6,1,65536]{3,2,1,0:T(2,128)(2,1)S(1)} %get-tuple-element.14, ...), kind=kLoop, calls=%fused_computation.16 | loop fusion | flops 6291456 | bytes 6291456 | tf_op jit(solution)/shard_map/stack | solution.py:68
  75.5 4.5 %pad_maximum_fusion = bf16[1,6,2,2,65536]{4,3,2,1,0:T(2,128)(2,1)S(1)} fusion(bf16[1,6,1,2,65536]{4,3,2,1,0:T(2,128)(2,1)S(1)} %get-tuple-element.32, bf16[1,6,1,2,65536]{4,3,2,1,0:T(2,128)(2,1)S(1)} %get-tuple-element.31), kind=kLoop, calls=%fused_computation | loop fusion | flops 1572864 | bytes 6291456 | tf_op jit(solution)/shard_map/stack | solution.py:68
  80.0 5.4 %convert_element_type.71 = bf16[12,2,256,256]{3,2,1,0:T(8,128)(2,1)} reshape(bf16[1,6,2,2,65536]{4,3,2,1,0:T(2,128)(2,1)S(1)} %pad_maximum_fusion) | data formatting | bytes 6291456 | tf_op jit(solution)/shard_map/convert_element_type | solution.py:68
  85.5 1.2 fusion.18
  86.7 0.0 copy-start.1
  86.7 3.8 %fusion.5 = f32[12,2,256,256]{2,3,1,0:T(8,128)S(1)} fusion(bf16[12,2,256,256]{3,2,1,0:T(8,128)(2,1)} %convert_element_type.71, bf16[1,2,256,256]{3,2,1,0:T(8,128)(2,1)S(1)} %get-tuple-element.19, bf16[1,2,256,256]{3,2,1,0:T(8,128)(2,1)S(1)} %get-tuple-element.24), kind=kOutput, calls=%fused_computation.9 | convolution fusion | flops 1611661312 | bytes 9961472 | tf_op jit(solution)/shard_map/oikn,binm->bokm/dot_general | solution.py:70
  90.5 0.0 copy-done.1
  90.5 0.9 add_convert_fusion
  91.4 4.5 %fusion.8 = f32[12,2,256,256]{3,2,0,1:T(8,128)} fusion(bf16[12,1,256,256]{2,3,1,0:T(8,128)(2,1)S(1)} %get-tuple-element.9, bf16[12,1,256,256]{2,3,1,0:T(8,128)(2,1)S(1)} %get-tuple-element.8, bf16[1,2,256,256]{3,2,1,0:T(8,128)(2,1)S(1)} %get-tuple-element.25, bf16[1,2,256,256]{3,2,1,0:T(8,128)(2,1)S(1)} %get-tuple-element.18), kind=kOutput, calls=%fused_computation.10 | convolution fusion | flops 1617166336 | bytes 9961472 | tf_op jit(solution)/shard_map/bikm,ioml->bolk/dot_general | solution.py:77
  95.8 10.9 %reshape.1140 = f32[1,6,2,2,65536]{4,2,1,3,0:T(2,128)} reshape(f32[12,2,256,256]{3,2,0,1:T(8,128)} %fusion.8) | data formatting | bytes 12582912 | tf_op jit(solution)/shard_map/reshape | solution.py:78
  106.8 0.0 copy-done
  106.8 0.0 copy-start.3
  106.8 0.0 copy-start.4
  106.8 0.0 copy-start.5
  106.8 9.9 %subtract_divide_fusion = f32[1,6,1,1,65536]{4,2,1,3,0:T(1,128)S(1)} fusion(f32[1,6,2,2,65536]{4,2,1,3,0:T(2,128)} %reshape.1140, f32[]{:T(128)} %bitcast.28, f32[]{:T(128)S(6)} %mul.738, f32[]{:T(128)} %add.192, f32[]{:T(128)} %add.186), kind=kLoop, calls=%fused_computation.18 | loop fusion | flops 5898240 | bytes 7864336 | tf_op jit(solution)/shard_map/div | solution.py:92
  116.8 0.0 copy-done.3
  116.8 1.3 add_bitcast_fusion
  118.1 10.2 %fusion.9 = f32[64,65536]{1,0:T(8,128)} fusion(f32[1,6,512,128]{3,2,1,0:T(8,128)S(1)} %add_bitcast_fusion, s32[64]{0:T(128)S(1)} %dynamic-slice_bitcast_fusion), kind=kOutput, calls=%fused_computation.11 | convolution fusion | flops 301990272 | bytes 18350336 | tf_op jit(solution)/shard_map/jsk,skf->jf/dot_general | solution.py:114
  128.3 0.0 reduce-scatter.2.cloned.1.call-update
  128.3 178.7 %reduce-scatter.2.cloned.1.call-done = f32[64,4096]{1,0:T(8,128)} async-done(((f32[64,65536]{1,0:T(8,128)}), f32[64,4096]{1,0:T(8,128)}) %reduce-scatter.2.cloned.1.call-update) | async-done | bytes 1048592 | tf_op jit(solution)/shard_map/reduce_scatter | solution.py:125
  307.0 2.3 broadcast_multiply_fusion
  (5 shorter events, 0.0 us)
Async XLA Ops:
  6.5 100.2 %copy-start = (s32[64,16]{0,1:T(8,128)S(1)}, s32[64,16]{0,1:T(8,128)}, u32[]{:S(2)}) copy-start(s32[64,16]{0,1:T(8,128)} %param.7) | copy-start | bytes 12292
  6.5 7.3 %copy-start.2 = (f32[1,2,65536]{2,1,0:T(2,128)S(1)}, f32[1,2,65536]{2,1,0:T(2,128)}, u32[]{:S(2)}) copy-start(f32[1,2,65536]{2,1,0:T(2,128)} %param.5) | copy-start | bytes 1572868
  6.5 300.5 %reduce-scatter.2.cloned.1.call-start = ((), (), s32[]{:S(2)}) async-start(), calls=%async_computation.1 | async-start | bytes 17825792 | tf_op jit(solution)/shard_map/reduce_scatter | solution.py:125
  86.7 3.8 %copy-start.1 = (f32[256,256]{0,1:T(8,128)S(1)}, f32[256,256]{0,1:T(8,128)}, u32[]{:S(2)}) copy-start(f32[256,256]{0,1:T(8,128)} %get-tuple-element.36) | copy-start | bytes 786436
  106.8 10.0 %copy-start.3 = (pred[6]{0:T(512)(128)(4,1)S(1)}, pred[6]{0:T(512)(128)(4,1)}, u32[]{:S(2)}) copy-start(pred[6]{0:T(512)(128)(4,1)} %get-tuple-element.28) | copy-start | bytes 22
  106.8 10.0 %copy-start.4 = (pred[6]{0:T(512)(128)(4,1)S(1)}, pred[6]{0:T(512)(128)(4,1)}, u32[]{:S(2)}) copy-start(pred[6]{0:T(512)(128)(4,1)} %get-tuple-element.29) | copy-start | bytes 22
  106.8 10.0 %copy-start.5 = (pred[6]{0:T(512)(128)(4,1)S(1)}, pred[6]{0:T(512)(128)(4,1)}, u32[]{:S(2)}) copy-start(pred[6]{0:T(512)(128)(4,1)} %get-tuple-element.30) | copy-start | bytes 22
Sparse Core Ops, SparseCore 0:
  128.4 178.5 reduce-scatter.1
where the time goes:
time: 319 us; the launch traced here: 316 us
  waiting for transfers between devices  179 us (56%)
  other arithmetic  85.7 us (27%)
  matrix products  18.4 us (6%)
  between operations  16.9 us (5%)
  local copies, waits for them, and re-layouts  16.4 us (5%)
    reduce_scatter x1, waiting for transfers between devices, local(): lax.psum_scatter(partial_sum, 'seg', scatter_dimension=1, tiled=True)  179 us
    another operation x4, other arithmetic  53.3 us
    another operation x2, other arithmetic, coherent_stat(): weighted = jnp.stack([with_a, with_b], 2).astype(jnp.bfloat16)  11.2 us
    reshape x1, local copies, waits for them, and re-layouts, coherent_stat(): spectra = spectra.reshape(seg_rows, KCOH, 2, 2, points)  10.9 us
    dot_general x1, matrix products, track_combine(): jnp.einsum('jsk,skf->jf', pick, moved, precision=lax.Precision.HIGHEST)  10.2 us
    div x1, other arithmetic, coherent_stat(): return energy / (points * determinant[:, None, None])  9.93 us
  transfers between devices with their start and end apart: 1, of which 1 were waited for; matrix products, arithmetic and copies ran while one was open for 0% of the time, Pallas kernels for 0%

commit v1 on v0

v1 whole, which is shorter than its diff:
```python
import functools
import math

import jax
import jax.numpy as jnp
import numpy as np
from jax import lax
from jax.experimental import pallas as pl
from jax.experimental.pallas import tpu as pltpu
from jax.sharding import PartitionSpec as P

BLK = 128
DMAX = 2
KCOH = 6
CHIRP_STEP = 3.0
TINY = 1e-06
PAD = 8
F32 = jnp.float32
BF16 = jnp.bfloat16


def dft_table(rows):
    index = np.arange(rows)
    angle = 2.0 * np.pi / rows * (index[:, None] * index[None, :] % rows)
    cos, sin = np.cos(angle), np.sin(angle)
    return jnp.asarray(np.block([[cos, sin], [-sin, cos]]), F32).astype(BF16)


def twist_table(rows):
    index = np.arange(rows)
    angle = 2.0 * np.pi / (rows * rows) * (index[:, None] * index[None, :])
    return jnp.asarray(np.stack([np.cos(angle), np.sin(angle)]), F32)


def chirp_table(rows, pairs):
    position = np.arange(rows * rows, dtype=np.float64) / (rows * rows)
    rates = (np.arange(KCOH) - (KCOH - 1) / 2.0) * CHIRP_STEP
    rates = np.array([rates[KCOH - 1 - pair] for pair in pairs])
    angle = 2.0 * np.pi * rates[:, None] * (position * position)[None, :]
    table = np.stack([np.cos(angle), np.sin(angle)], 1)
    return jnp.asarray(table.reshape(len(pairs), 2, rows, rows), F32)


def stat_kernel(
    pairs, count, drift, series, weights, table, twist, chirp, out, lanes, prep, coef, moved
):
    rows = table.shape[0] // 2
    halves = rows // BLK
    step = pl.program_id(0)
    me = lax.axis_index("seg")
    core, chip = lax.rem(me, 2), lax.div(me, 2)

    def take(ref, row):
        pieces = [
            ref[pl.ds(2 * half + row, rows, stride=2 * halves), :] for half in range(halves)
        ]
        return jnp.concatenate(pieces, axis=1)

    @pl.when(step == 0)
    def _():
        lanes[...] = series[...].astype(F32)
        real, imag = take(lanes, 0), take(lanes, 1)
        first, second = take(weights, 0), take(weights, 1)
        prep[0] = first * real
        prep[1] = first * imag
        prep[2] = second * real
        prep[3] = second * imag
        points = rows * rows
        aa = jnp.sum(first * first) / points + TINY
        bb = jnp.sum(second * second) / points + TINY
        ab = jnp.sum(first * second) / points
        det = jnp.maximum(aa * bb - ab * ab, 0.1 * aa * bb)
        scale = points * det
        coef[0] = bb / scale
        coef[1] = aa / scale
        coef[2] = 2.0 * ab / scale

    cos, sin = chirp[0, 0], chirp[0, 1]
    turn_cos, turn_sin = twist[0], twist[1]
    turned = []
    for weight in range(2):
        real, imag = prep[2 * weight], prep[2 * weight + 1]
        turned.append((real * cos, imag * sin, imag * cos, real * sin))
    pair = step * 0
    for position, value in enumerate(pairs):
        pair = jnp.where(step == position, value, pair)
    for side in range(2):
        sign = 1.0 if side == 0 else -1.0
        left = jnp.concatenate([rc + sign * iS for rc, iS, _, _ in turned], axis=1)
        right = jnp.concatenate([ic - sign * rs for _, _, ic, rs in turned], axis=1)
        weighted = jnp.concatenate([left.astype(BF16), right.astype(BF16)], axis=0)
        one = jnp.dot(table[...], weighted, preferred_element_type=F32)
        spectra = []
        for weight in range(2):
            columns = slice(weight * rows, (weight + 1) * rows)
            one_real, one_imag = one[:rows, columns], one[rows:, columns]
            middle = jnp.concatenate(
                [
                    (one_real * turn_cos + one_imag * turn_sin).astype(BF16),
                    (one_imag * turn_cos - one_real * turn_sin).astype(BF16),
                ],
                axis=1,
            )
            both = lax.dot_general(
                table[...], middle, (((1,), (1,)), ((), ())), preferred_element_type=F32
            )
            spectra += [both[:rows], both[rows:]]
        ar, ai, br, bi = spectra
        energy = (
            coef[0] * (ar * ar + ai * ai)
            + coef[1] * (br * br + bi * bi)
            - coef[2] * (ar * br + ai * bi)
        )
        amount = drift[0, KCOH - 1 - pair] if side == 0 else drift[0, pair]
        moved[PAD : PAD + PAD] = jnp.zeros((PAD, BLK), F32)
        moved[PAD + halves * rows - PAD : PAD + halves * rows] = jnp.zeros((PAD, BLK), F32)
        for half in range(halves):
            moved[pl.ds(PAD + half + amount, rows, stride=halves), :] = energy[
                :, half * BLK : (half + 1) * BLK
            ]
        per = halves * rows // count
        for dest in range(count):
            other = lax.bitwise_xor(dest % 2, core)
            away = lax.bitwise_xor(dest // 2, chip)
            out[0, other, away, side] = moved[PAD + dest * per : PAD + (dest + 1) * per]


def stat(pairs, count, drift, series, weights):
    points = series.shape[0] * BLK // 2
    rows = math.isqrt(points)
    per = points // BLK // count
    shape = (len(pairs), 2, count // 2, 2, per, BLK)
    whole = lambda shape: pl.BlockSpec(shape, lambda step: (0,) * len(shape))
    return pl.pallas_call(
        functools.partial(stat_kernel, pairs, count),
        grid=(len(pairs),),
        out_shape=jax.ShapeDtypeStruct(shape, F32),
        in_specs=[
            pl.BlockSpec(memory_space=pltpu.SMEM),
            whole(series.shape),
            whole(weights.shape),
            whole((2 * rows, 2 * rows)),
            whole((2, rows, rows)),
            pl.BlockSpec((1, 2, rows, rows), lambda step: (step, 0, 0, 0)),
        ],
        out_specs=pl.BlockSpec((1,) + shape[1:], lambda step: (step, 0, 0, 0, 0, 0)),
        scratch_shapes=[
            pltpu.VMEM(series.shape, F32),
            pltpu.VMEM((4, rows, rows), F32),
            pltpu.SMEM((3,), F32),
            pltpu.VMEM((points // BLK + 2 * PAD, BLK), F32),
        ],
        compiler_params=pltpu.CompilerParams(vmem_limit_bytes=48 * 2**20),
    )(drift, series, weights, dft_table(rows), twist_table(rows), chirp_table(rows, pairs))


def sum_kernel(height, segments, tracks, meta, *refs):
    blocks, out, gathered = refs[:-2], refs[-2], refs[-1]
    per = blocks[0].shape[0] // height
    me = lax.axis_index("seg")
    core, chip = lax.rem(me, 2), lax.div(me, 2)
    level, other, away = meta[0:1], meta[1:2], meta[2:3]
    segment = 2 * lax.bitwise_xor(away, chip) + lax.bitwise_xor(other, core)
    places = lax.broadcasted_iota(jnp.int32, (segments, meta.shape[1]), 0)
    chosen = (places == segment).astype(F32).astype(BF16)
    named = jnp.dot(
        tracks[...].astype(F32).astype(BF16), chosen, preferred_element_type=F32
    )
    pick = jnp.where((named == level.astype(F32)) | (level < 0), 1.0, 0.0).astype(BF16)
    for column in range(per):
        for index, block in enumerate(blocks):
            gathered[index * height : (index + 1) * height, column * BLK : (column + 1) * BLK] = (
                block[pl.ds(column, height, stride=per), :]
            )
    for column in range(0, per * BLK, 512):
        width = min(512, per * BLK - column)
        value = gathered[:, column : column + width]
        high = value.astype(BF16)
        low = (value - high.astype(F32)).astype(BF16)
        total = jnp.dot(pick, high, preferred_element_type=F32)
        total = total + jnp.dot(pick, low, preferred_element_type=F32)
        out[:, column : column + width] = total * (1.0 / segments)


def track_sum(tracks, levels, blocks):
    height = len(levels)
    ntrack, segments = tracks.shape
    per = blocks[0].shape[0] // height
    meta = np.array(
        [
            [level, other, away]
            for away in range(len(blocks))
            for level, other in levels
        ]
    ).T
    return pl.pallas_call(
        functools.partial(sum_kernel, height, segments),
        out_shape=jax.ShapeDtypeStruct((ntrack, per * BLK), F32),
        scratch_shapes=[pltpu.VMEM((len(blocks) * height, per * BLK), F32)],
        compiler_params=pltpu.CompilerParams(vmem_limit_bytes=48 * 2**20),
    )(tracks, jnp.asarray(meta, jnp.int32), *blocks)


def local(count, strain_series, antenna, drift, tracks):
    points = strain_series.shape[2]
    tile = lambda array: array.reshape(2, points // BLK, BLK).transpose(1, 0, 2).reshape(-1, BLK)
    series, weights = tile(strain_series), tile(antenna)
    pairs = tuple(range(KCOH // 2))
    stats = stat(pairs, count, drift, series, weights)
    swap = lambda hop: [(device, device ^ hop) for device in range(count)]
    mine = stats[:, 0]
    got = lax.ppermute(stats[:, 1], "seg", swap(1))
    base = mine[0, :, 0] + got[0, :, 0]
    levels, rows = [(-1, 0)], [base]
    for other, part in enumerate((mine, got)):
        for pair in pairs:
            for side in range(2):
                level = pair if side else KCOH - 1 - pair
                if (pair, side) != (0, 0):
                    levels.append((level, other))
                    rows.append(part[pair, :, side] - part[0, :, 0])
    packed = jnp.stack(rows, 1)
    packed = packed.reshape(packed.shape[0], -1, BLK)
    blocks = [packed[0]]
    for away in range(1, count // 2):
        blocks.append(lax.ppermute(packed[away], "seg", swap(2 * away)))
    return track_sum(tracks, levels, blocks)


def solution(mesh):
    return jax.shard_map(
        functools.partial(local, mesh.shape["seg"]),
        mesh=mesh,
        in_specs=(
            P(("sky", "seg"), None, None),
            P(("sky", "seg"), None, None),
            P(("sky", "seg"), None),
            P(),
        ),
        out_specs=P("sky", "seg"),
        check_vma=False,
    )
```

time: 319 us -> 57 us (0.18)
  waiting for transfers between devices: 179 us -> 32.6 us
  other arithmetic: 85.7 us -> 0.22 us
  matrix products: 18.4 us -> 0 us
  between operations: 16.9 us -> 0.15 us
  local copies, waits for them, and re-layouts: 16.4 us -> 6.58 us
  Pallas kernels: 0 us -> 9.22 us
  starting transfers between devices: 0.01 us -> 7.96 us
    reduce_scatter x1 -> x0, waiting for transfers between devices: 179 us -> none  [local(): lax.psum_scatter(partial_sum, 'seg', scatter_dimension=1, tiled=True)]
    another operation x7 -> x1, other arithmetic: 65.7 us -> 0.02 us  [local(): packed = jnp.stack(rows, 1)]
    ppermute x0 -> x8, waiting for transfers between devices: none -> 32.6 us  [the longest x7 30.4 us: local(): blocks.append(lax.ppermute(packed[away], 'seg', swap(2 * away)))]
    dot_general x3 -> x0, matrix products: 18.4 us -> none  [the longest x1 10.2 us: track_combine(): jnp.einsum('jsk,skf->jf', pick, moved, precision=lax.Precision.HIGHEST)]
    div x2 -> x0, other arithmetic: 12.2 us -> none  [the longest x1 9.93 us: coherent_stat(): return energy / (points * determinant[:, None, None])]
    reshape x1 -> x0, local copies, waits for them, and re-layouts: 10.9 us -> none  [coherent_stat(): spectra = spectra.reshape(seg_rows, KCOH, 2, 2, points)]
    pallas_call x0 -> x2, Pallas kernels: none -> 9.22 us  [the longest x1 6.74 us: stat(): pl.pallas_call(functools.partial(stat_kernel, pairs, count), grid=(len(pa...]
    ppermute x0 -> x8, starting transfers between devices: none -> 7.96 us  [the longest x7 7.88 us: local(): blocks.append(lax.ppermute(packed[away], 'seg', swap(2 * away)))]
  transfers between devices with their start and end apart: 1 -> 8, of which waited for: 1 -> 7; matrix products, arithmetic and copies ran while one was open for 0% -> 0% of each run, Pallas kernels for 0% -> 0%
where the time goes in v1:
time: 57 us; the launch traced here: 56.7 us
  waiting for transfers between devices  32.6 us (57%)
  Pallas kernels  9.22 us (16%)
  starting transfers between devices  7.96 us (14%)
  local copies, waits for them, and re-layouts  6.58 us (12%)
    ppermute x7, waiting for transfers between devices, local(): blocks.append(lax.ppermute(packed[away], 'seg', swap(2 * away)))  30.4 us
    ppermute x7, starting transfers between devices, local(): blocks.append(lax.ppermute(packed[away], 'seg', swap(2 * away)))  7.88 us
    pallas_call x1, Pallas kernels, stat(): pl.pallas_call(functools.partial(stat_kernel, pairs, count), grid=(len(pa...  6.74 us
    unnamed x18, local copies, waits for them, and re-layouts  6.29 us
    pallas_call x1, Pallas kernels, track_sum(): pl.pallas_call(functools.partial(sum_kernel, height, segments), out_shape...  2.48 us
    ppermute x1, waiting for transfers between devices, local(): got = lax.ppermute(stats[:, 1], 'seg', swap(1))  2.21 us
  transfers between devices with their start and end apart: 8, of which 7 were waited for; matrix products, arithmetic and copies ran while one was open for 0% of the time, Pallas kernels for 0%

profile of v1, /device:TPU:16, one launch (start us, length us, event | category | flops | bytes accessed | tf_op | source)
XLA Modules:
  0.0 56.7 jit_solution(11836885655255657232)
XLA Ops:
  0.0 1.4 %copy-done = f32[3,2,256,256]{3,2,1,0:T(8,128)S(1)} copy-done((f32[3,2,256,256]{3,2,1,0:T(8,128)S(1)}, f32[3,2,256,256]{3,2,1,0:T(8,128)}, u32[]{:S(2)}) %copy-start) | copy-done | bytes 1572888
  1.4 1.0 %copy-done.1 = f32[1,2,65536]{2,1,0:T(2,128)S(1)} copy-done((f32[1,2,65536]{2,1,0:T(2,128)S(1)}, f32[1,2,65536]{2,1,0:T(2,128)}, u32[]{:S(2)}) %copy-start.1) | copy-done | bytes 524312
  2.5 1.0 %copy-done.2 = bf16[512,512]{1,0:T(8,128)(2,1)S(1)} copy-done((bf16[512,512]{1,0:T(8,128)(2,1)S(1)}, bf16[512,512]{1,0:T(8,128)(2,1)}, u32[]{:S(2)}) %copy-start.2) | copy-done | bytes 524312
  3.5 1.0 %copy-done.3 = f32[2,256,256]{2,1,0:T(8,128)S(1)} copy-done((f32[2,256,256]{2,1,0:T(8,128)S(1)}, f32[2,256,256]{2,1,0:T(8,128)}, u32[]{:S(2)}) %copy-start.3) | copy-done | bytes 524312
  4.5 0.9 %copy-done.4 = bf16[1,2,65536]{2,1,0:T(2,128)(2,1)S(1)} copy-done((bf16[1,2,65536]{2,1,0:T(2,128)(2,1)S(1)}, bf16[1,2,65536]{2,1,0:T(2,128)(2,1)}, u32[]{:S(2)}) %copy-start.4) | copy-done | bytes 262168
  5.5 0.7 %copy-done.6 = s32[1,6]{1,0:T(1,128)S(1)} copy-done((s32[1,6]{1,0:T(1,128)S(1)}, s32[1,6]{1,0:T(1,128)}, u32[]{:S(2)}) %copy-start.6) | copy-done | bytes 48
  6.1 6.7 %shard_map.82 = f32[3,2,8,2,32,128]{5,4,3,2,1,0:T(8,128)S(1)} custom-call(s32[1,6]{1,0:T(1,128)S(1)} %copy-done.6, bf16[1024,128]{1,0:T(8,128)(2,1)S(1)} %bitcast.113, f32[1024,128]{1,0:T(8,128)S(1)} %bitcast.112, bf16[512,512]{1,0:T(8,128)(2,1)S(1)} %copy-done.2, f32[2,256,256]{2,1,0:T(8,128)S(1)} %copy-done.3, f32[3,2,256,256]{3,2,1,0:T(8,128)S(1)} %copy-done), custom_call_target="tpu_custom_call" | custom-call | tf_op jit(solution)/shard_map/pallas_call | solution.py:134
  12.9 0.2 fusion.26
  13.1 0.1 collective-permute-start
  13.1 0.1 copy.26
  13.2 2.2 %collective-permute-done = f32[3,8,2,32,128]{4,3,2,1,0:T(8,128)S(1)} collective-permute-done((f32[3,8,2,32,128]{4,3,2,1,0:T(8,128)S(1)}, f32[3,8,2,32,128]{4,3,2,1,0:T(8,128)S(1)}, u32[]{:S(2)}, u32[]{:S(2)}) %collective-permute-start) | collective-permute-done | bytes 786464 | tf_op jit(solution)/shard_map/ppermute | solution.py:212
  15.7 0.0 copy-start.7
  15.7 0.0 copy-start.5
  15.7 0.1 fusion.27
  15.9 1.6 %collective-permute-start.1 = (f32[352,128]{1,0:T(8,128)S(1)}, f32[352,128]{1,0:T(8,128)S(1)}, u32[]{:S(2)}, u32[]{:S(2)}) collective-permute-start(f32[352,128]{1,0:T(8,128)S(1)} %bitcast.126), channel_id=1, source_target_pairs={{0,2},{1,3},{2,0},{3,1},{4,6},{5,7},{6,4},{7,5},{8,10},{9,11},{10,... | collective-permute-start | bytes 540680 | tf_op jit(solution)/shard_map/ppermute | solution.py:226
  17.5 1.6 %collective-permute-start.2 = (f32[352,128]{1,0:T(8,128)S(1)}, f32[352,128]{1,0:T(8,128)S(1)}, u32[]{:S(2)}, u32[]{:S(2)}) collective-permute-start(f32[352,128]{1,0:T(8,128)S(1)} %bitcast.125), channel_id=1, source_target_pairs={{0,4},{1,5},{2,6},{3,7},{4,0},{5,1},{6,2},{7,3},{8,12},{9,13},{10,... | collective-permute-start | bytes 540680 | tf_op jit(solution)/shard_map/ppermute | solution.py:226
  19.0 0.4 collective-permute-start.3
  19.4 0.0 collective-permute-start.4
  19.4 3.9 %collective-permute-start.5 = (f32[352,128]{1,0:T(8,128)S(1)}, f32[352,128]{1,0:T(8,128)S(1)}, u32[]{:S(2)}, u32[]{:S(2)}) collective-permute-start(f32[352,128]{1,0:T(8,128)S(1)} %bitcast.122), channel_id=1, source_target_pairs={{0,10},{1,11},{2,8},{3,9},{4,14},{5,15},{6,12},{7,13},{8,2},{9,3},... | collective-permute-start | bytes 540680 | tf_op jit(solution)/shard_map/ppermute | solution.py:226
  23.3 0.0 collective-permute-done.1.refs_1_
  23.3 0.4 collective-permute-start.6
  23.8 5.5 %collective-permute-done.2.refs_2_ = f32[352,128]{1,0:T(8,128)S(1)} collective-permute-done((f32[352,128]{1,0:T(8,128)S(1)}, f32[352,128]{1,0:T(8,128)S(1)}, u32[]{:S(2)}, u32[]{:S(2)}) %collective-permute-start.2) | collective-permute-done | bytes 180256 | tf_op jit(solution)/shard_map/ppermute | solution.py:226
  29.2 0.0 collective-permute-start.7
  29.2 0.0 copy-done.7
  29.2 0.1 copy.18.tracks
  29.3 2.6 %collective-permute-done.3.refs_3_ = f32[352,128]{1,0:T(8,128)S(1)} collective-permute-done((f32[352,128]{1,0:T(8,128)S(1)}, f32[352,128]{1,0:T(8,128)S(1)}, u32[]{:S(2)}, u32[]{:S(2)}) %collective-permute-start.3) | collective-permute-done | bytes 180256 | tf_op jit(solution)/shard_map/ppermute | solution.py:226
  32.0 0.6 %collective-permute-done.4.refs_4_ = f32[352,128]{1,0:T(8,128)S(1)} collective-permute-done((f32[352,128]{1,0:T(8,128)S(1)}, f32[352,128]{1,0:T(8,128)S(1)}, u32[]{:S(2)}, u32[]{:S(2)}) %collective-permute-start.4) | collective-permute-done | bytes 180256 | tf_op jit(solution)/shard_map/ppermute | solution.py:226
  32.6 11.2 %collective-permute-done.5.refs_5_ = f32[352,128]{1,0:T(8,128)S(1)} collective-permute-done((f32[352,128]{1,0:T(8,128)S(1)}, f32[352,128]{1,0:T(8,128)S(1)}, u32[]{:S(2)}, u32[]{:S(2)}) %collective-permute-start.5) | collective-permute-done | bytes 180256 | tf_op jit(solution)/shard_map/ppermute | solution.py:226
  43.8 7.3 %collective-permute-done.6.refs_6_ = f32[352,128]{1,0:T(8,128)S(1)} collective-permute-done((f32[352,128]{1,0:T(8,128)S(1)}, f32[352,128]{1,0:T(8,128)S(1)}, u32[]{:S(2)}, u32[]{:S(2)}) %collective-permute-start.6) | collective-permute-done | bytes 180256 | tf_op jit(solution)/shard_map/ppermute | solution.py:226
  51.1 3.1 %collective-permute-done.7.refs_7_ = f32[352,128]{1,0:T(8,128)S(1)} collective-permute-done((f32[352,128]{1,0:T(8,128)S(1)}, f32[352,128]{1,0:T(8,128)S(1)}, u32[]{:S(2)}, u32[]{:S(2)}) %collective-permute-start.7) | collective-permute-done | bytes 180256 | tf_op jit(solution)/shard_map/ppermute | solution.py:226
  54.2 0.0 copy-done.5
  54.2 2.5 %shard_map.83 = f32[64,4096]{1,0:T(8,128)} custom-call(s32[64,16]{1,0:T(8,128)S(1)} %copy.18.tracks, s32[3,88]{1,0:T(4,128)S(1)} %copy-done.5, f32[352,128]{1,0:T(8,128)S(1)} %bitcast.111, f32[352,128]{1,0:T(8,128)S(1)} %collective-permute-done.1.refs_1_, f32[352,128]{1,0:T(8,128)S(1)} %collective-permute-done.2.refs_2_, ...), custom_call_target="tpu_custom_call" | custom-call | tf_op jit(solution)/shard_map/pallas_call | solution.py:196
  (17 shorter events, 0.2 us)
Async XLA Ops:
  0.0 1.4 %copy-start = (f32[3,2,256,256]{3,2,1,0:T(8,128)S(1)}, f32[3,2,256,256]{3,2,1,0:T(8,128)}, u32[]{:S(2)}) copy-start(f32[3,2,256,256]{3,2,1,0:T(8,128)} %constant.10.clone.chirp) | copy-start | bytes 4718596
  1.4 1.0 %copy-start.1 = (f32[1,2,65536]{2,1,0:T(2,128)S(1)}, f32[1,2,65536]{2,1,0:T(2,128)}, u32[]{:S(2)}) copy-start(f32[1,2,65536]{2,1,0:T(2,128)} %param.9) | copy-start | bytes 1572868
  2.5 1.0 %copy-start.2 = (bf16[512,512]{1,0:T(8,128)(2,1)S(1)}, bf16[512,512]{1,0:T(8,128)(2,1)}, u32[]{:S(2)}) copy-start(bf16[512,512]{1,0:T(8,128)(2,1)} %constant.15.table) | copy-start | bytes 1572868
  3.5 1.0 %copy-start.3 = (f32[2,256,256]{2,1,0:T(8,128)S(1)}, f32[2,256,256]{2,1,0:T(8,128)}, u32[]{:S(2)}) copy-start(f32[2,256,256]{2,1,0:T(8,128)} %constant.9.clone.twist) | copy-start | bytes 1572868
  4.5 0.9 %copy-start.4 = (bf16[1,2,65536]{2,1,0:T(2,128)(2,1)S(1)}, bf16[1,2,65536]{2,1,0:T(2,128)(2,1)}, u32[]{:S(2)}) copy-start(bf16[1,2,65536]{2,1,0:T(2,128)(2,1)} %param.8) | copy-start | bytes 786436
  5.5 0.7 %copy-start.6 = (s32[1,6]{1,0:T(1,128)S(1)}, s32[1,6]{1,0:T(1,128)}, u32[]{:S(2)}) copy-start(s32[1,6]{1,0:T(1,128)} %drift.1) | copy-start | bytes 76
  13.1 2.4 %collective-permute-start = (f32[3,8,2,32,128]{4,3,2,1,0:T(8,128)S(1)}, f32[3,8,2,32,128]{4,3,2,1,0:T(8,128)S(1)}, u32[]{:S(2)}, u32[]{:S(2)}) collective-permute-start(f32[3,8,2,32,128]{4,3,2,1,0:T(8,128)S(1)} %get-tuple-element.6), channel_id=1, source_target_pairs={{0,1},{1,0},{2,3},{3,2},{4,5},{5,4},{6,7},{7,6},{8,9},{9,8},{10,11... | collective-permute-start | bytes 2359304 | tf_op jit(solution)/shard_map/ppermute | solution.py:212
  15.7 13.5 %copy-start.7 = (s32[64,16]{0,1:T(8,128)S(1)}, s32[64,16]{0,1:T(8,128)}, u32[]{:S(2)}) copy-start(s32[64,16]{0,1:T(8,128)} %param.11) | copy-start | bytes 12292
  15.7 38.5 %copy-start.5 = (s32[3,88]{1,0:T(4,128)S(1)}, s32[3,88]{1,0:T(4,128)}, u32[]{:S(2)}) copy-start(s32[3,88]{1,0:T(4,128)} %constant.11.clone.meta) | copy-start | bytes 3172
  15.9 7.4 %collective-permute-start.1 = (f32[352,128]{1,0:T(8,128)S(1)}, f32[352,128]{1,0:T(8,128)S(1)}, u32[]{:S(2)}, u32[]{:S(2)}) collective-permute-start(f32[352,128]{1,0:T(8,128)S(1)} %bitcast.126), channel_id=1, source_target_pairs={{0,2},{1,3},{2,0},{3,1},{4,6},{5,7},{6,4},{7,5},{8,10},{9,11},{10,... | collective-permute-start | bytes 540680 | tf_op jit(solution)/shard_map/ppermute | solution.py:226
  17.5 11.8 %collective-permute-start.2 = (f32[352,128]{1,0:T(8,128)S(1)}, f32[352,128]{1,0:T(8,128)S(1)}, u32[]{:S(2)}, u32[]{:S(2)}) collective-permute-start(f32[352,128]{1,0:T(8,128)S(1)} %bitcast.125), channel_id=1, source_target_pairs={{0,4},{1,5},{2,6},{3,7},{4,0},{5,1},{6,2},{7,3},{8,12},{9,13},{10,... | collective-permute-start | bytes 540680 | tf_op jit(solution)/shard_map/ppermute | solution.py:226
  19.0 12.9 %collective-permute-start.3 = (f32[352,128]{1,0:T(8,128)S(1)}, f32[352,128]{1,0:T(8,128)S(1)}, u32[]{:S(2)}, u32[]{:S(2)}) collective-permute-start(f32[352,128]{1,0:T(8,128)S(1)} %bitcast.124), channel_id=1, source_target_pairs={{0,6},{1,7},{2,4},{3,5},{4,2},{5,3},{6,0},{7,1},{8,14},{9,15},{10,... | collective-permute-start | bytes 540680 | tf_op jit(solution)/shard_map/ppermute | solution.py:226
  19.4 13.2 %collective-permute-start.4 = (f32[352,128]{1,0:T(8,128)S(1)}, f32[352,128]{1,0:T(8,128)S(1)}, u32[]{:S(2)}, u32[]{:S(2)}) collective-permute-start(f32[352,128]{1,0:T(8,128)S(1)} %bitcast.123), channel_id=1, source_target_pairs={{0,8},{1,9},{2,10},{3,11},{4,12},{5,13},{6,14},{7,15},{8,0},{9,1},... | collective-permute-start | bytes 540680 | tf_op jit(solution)/shard_map/ppermute | solution.py:226
  19.4 24.3 %collective-permute-start.5 = (f32[352,128]{1,0:T(8,128)S(1)}, f32[352,128]{1,0:T(8,128)S(1)}, u32[]{:S(2)}, u32[]{:S(2)}) collective-permute-start(f32[352,128]{1,0:T(8,128)S(1)} %bitcast.122), channel_id=1, source_target_pairs={{0,10},{1,11},{2,8},{3,9},{4,14},{5,15},{6,12},{7,13},{8,2},{9,3},... | collective-permute-start | bytes 540680 | tf_op jit(solution)/shard_map/ppermute | solution.py:226
  23.3 27.8 %collective-permute-start.6 = (f32[352,128]{1,0:T(8,128)S(1)}, f32[352,128]{1,0:T(8,128)S(1)}, u32[]{:S(2)}, u32[]{:S(2)}) collective-permute-start(f32[352,128]{1,0:T(8,128)S(1)} %bitcast.121), channel_id=1, source_target_pairs={{0,12},{1,13},{2,14},{3,15},{4,8},{5,9},{6,10},{7,11},{8,4},{9,5},... | collective-permute-start | bytes 540680 | tf_op jit(solution)/shard_map/ppermute | solution.py:226
  29.2 25.0 %collective-permute-start.7 = (f32[352,128]{1,0:T(8,128)S(1)}, f32[352,128]{1,0:T(8,128)S(1)}, u32[]{:S(2)}, u32[]{:S(2)}) collective-permute-start(f32[352,128]{1,0:T(8,128)S(1)} %bitcast.120), channel_id=1, source_target_pairs={{0,14},{1,15},{2,12},{3,13},{4,10},{5,11},{6,8},{7,9},{8,6},{9,7},... | collective-permute-start | bytes 540680 | tf_op jit(solution)/shard_map/ppermute | solution.py:226

commit v2 on v1

v2 whole, which is shorter than its diff:
```python
import functools
import math

import jax
import jax.numpy as jnp
import numpy as np
from jax import lax
from jax.experimental import pallas as pl
from jax.experimental.pallas import tpu as pltpu
from jax.sharding import PartitionSpec as P

BLK = 128
DMAX = 2
KCOH = 6
CHIRP_STEP = 3.0
TINY = 1e-06
PAD = 8
F32 = jnp.float32
BF16 = jnp.bfloat16


def dft_table(rows):
    index = np.arange(rows)
    angle = 2.0 * np.pi / rows * (index[:, None] * index[None, :] % rows)
    cos, sin = np.cos(angle), np.sin(angle)
    return jnp.asarray(np.block([[cos, sin], [-sin, cos]]), F32).astype(BF16)


def twist_table(rows):
    index = np.arange(rows)
    angle = 2.0 * np.pi / (rows * rows) * (index[:, None] * index[None, :])
    return jnp.asarray(np.stack([np.cos(angle), np.sin(angle)]), F32)


def chirp_table(rows, pairs):
    position = np.arange(rows * rows, dtype=np.float64) / (rows * rows)
    rates = (np.arange(KCOH) - (KCOH - 1) / 2.0) * CHIRP_STEP
    rates = np.array([rates[KCOH - 1 - pair] for pair in pairs])
    angle = 2.0 * np.pi * rates[:, None] * (position * position)[None, :]
    table = np.stack([np.cos(angle), np.sin(angle)], 1)
    return jnp.asarray(table.reshape(len(pairs), 2, rows, rows), F32)


def split_segment(weights, lanes, prep, coef):
    rows = prep.shape[1]
    halves = rows // BLK

    def take(ref, row):
        pieces = [
            ref[pl.ds(2 * half + row, rows, stride=2 * halves), :] for half in range(halves)
        ]
        return jnp.concatenate(pieces, axis=1)

    real, imag = take(lanes, 0), take(lanes, 1)
    first, second = take(weights, 0), take(weights, 1)
    prep[0] = first * real
    prep[1] = first * imag
    prep[2] = second * real
    prep[3] = second * imag
    points = rows * rows
    aa = jnp.sum(first * first) / points + TINY
    bb = jnp.sum(second * second) / points + TINY
    ab = jnp.sum(first * second) / points
    det = jnp.maximum(aa * bb - ab * ab, 0.1 * aa * bb)
    scale = points * det
    coef[0] = bb / scale
    coef[1] = aa / scale
    coef[2] = 2.0 * ab / scale


def one_stat(pair, side, drift, chirp, table, twist, prep, coef, moved):
    rows = table.shape[0] // 2
    halves = rows // BLK
    sign = 1.0 if side == 0 else -1.0
    cos, sin = chirp[0], chirp[1] * sign
    left = jnp.concatenate([prep[2 * w] * cos + prep[2 * w + 1] * sin for w in (0, 1)], axis=1)
    right = jnp.concatenate([prep[2 * w + 1] * cos - prep[2 * w] * sin for w in (0, 1)], axis=1)
    weighted = jnp.concatenate([left.astype(BF16), right.astype(BF16)], axis=0)
    one = jnp.dot(table[...], weighted, preferred_element_type=F32)
    turn_cos, turn_sin = twist[0], twist[1]
    spectra = []
    for weight in range(2):
        columns = slice(weight * rows, (weight + 1) * rows)
        one_real, one_imag = one[:rows, columns], one[rows:, columns]
        middle = jnp.concatenate(
            [
                (one_real * turn_cos + one_imag * turn_sin).astype(BF16),
                (one_imag * turn_cos - one_real * turn_sin).astype(BF16),
            ],
            axis=1,
        )
        both = lax.dot_general(
            table[...], middle, (((1,), (1,)), ((), ())), preferred_element_type=F32
        )
        spectra += [both[:rows], both[rows:]]
    ar, ai, br, bi = spectra
    energy = (
        coef[0] * (ar * ar + ai * ai)
        + coef[1] * (br * br + bi * bi)
        - coef[2] * (ar * br + ai * bi)
    )
    amount = drift[0, level_of(pair, side)]
    moved[PAD : PAD + PAD] = jnp.zeros((PAD, BLK), F32)
    moved[PAD + halves * rows - PAD : PAD + halves * rows] = jnp.zeros((PAD, BLK), F32)
    for half in range(halves):
        moved[pl.ds(PAD + half + amount, rows, stride=halves), :] = energy[
            :, half * BLK : (half + 1) * BLK
        ]


def level_of(pair, side):
    return pair if side else KCOH - 1 - pair


def block_of(count, per, away, other):
    me = lax.axis_index("seg")
    core, chip = lax.rem(me, 2), lax.div(me, 2)
    dest = 2 * lax.bitwise_xor(chip, away) + lax.bitwise_xor(core, other)
    return pl.ds(pl.multiple_of(PAD + dest * per, math.gcd(per, PAD)), per)


EARLY = ((1, 0), (1, 1), (0, 0), (0, 1), (2, 0), (2, 1))


def fetch(pairs, sems):
    moves = [
        pltpu.make_async_copy(source, target, sems.at[index])
        for index, (source, target) in enumerate(pairs)
    ]
    for move in moves:
        move.start()
    return moves


def stat_kernel(
    kept, count, drift, series_hbm, weights_hbm, table_hbm, twist_hbm, chirp_hbm,
    own_hbm, give_hbm,
    series, weights, table, twist, chirp, lanes, prep, coef, moved, own, give, sems, out_sems,
):
    first_pair = min(pair for pair, _ in kept)
    moves = fetch(
        [
            (series_hbm, series),
            (weights_hbm, weights),
            (chirp_hbm, chirp),
            (table_hbm, table),
            (twist_hbm, twist),
        ],
        sems,
    )
    moves[0].wait()
    lanes[...] = series[...].astype(F32)
    moves[1].wait()
    split_segment(weights, lanes, prep, coef)
    for move in moves[2:]:
        move.wait()
    per = own.shape[2]
    outs = []
    for index, (pair, side) in enumerate(kept):
        at = chirp.at[pair - first_pair]
        one_stat(pair, side, drift, at, table, twist, prep, coef, moved)
        for other, (held, target) in enumerate(((give, give_hbm), (own, own_hbm))):
            for away in range(count // 2):
                held[index, away] = moved[block_of(count, per, away, 1 - other), :]
            outs.append(
                pltpu.make_async_copy(
                    held.at[index], target.at[index], out_sems.at[2 * index + other]
                )
            )
            outs[-1].start()
    for out in outs:
        out.wait()


def stat(kept, limit, cost, count, drift, series, weights):
    points = series.shape[0] * BLK // 2
    rows = math.isqrt(points)
    per = points // BLK // count
    chips = count // 2
    pairs = tuple(sorted({pair for pair, _ in kept}))
    hbm = pl.BlockSpec(memory_space=pltpu.HBM)
    smem = pl.BlockSpec(memory_space=pltpu.SMEM)
    shape = (len(kept), chips, per, BLK)
    return pl.pallas_call(
        functools.partial(stat_kernel, kept, count),
        out_shape=(jax.ShapeDtypeStruct(shape, F32),) * 2,
        in_specs=[smem] + [hbm] * 5,
        out_specs=(hbm, hbm),
        scratch_shapes=[
            pltpu.VMEM(series.shape, BF16),
            pltpu.VMEM(weights.shape, F32),
            pltpu.VMEM((2 * rows, 2 * rows), BF16),
            pltpu.VMEM((2, rows, rows), F32),
            pltpu.VMEM((len(pairs), 2, rows, rows), F32),
            pltpu.VMEM(series.shape, F32),
            pltpu.VMEM((4, rows, rows), F32),
            pltpu.SMEM((3,), F32),
            pltpu.VMEM((points // BLK + 2 * PAD, BLK), F32),
            pltpu.VMEM(shape, F32),
            pltpu.VMEM(shape, F32),
            pltpu.SemaphoreType.DMA((5,)),
            pltpu.SemaphoreType.DMA((2 * len(kept),)),
        ],
        compiler_params=pltpu.CompilerParams(vmem_limit_bytes=limit * 2**20),
        cost_estimate=pl.CostEstimate(flops=cost, bytes_accessed=3 * 2**20, transcendentals=0),
    )(drift, series, weights, dft_table(rows), twist_table(rows), chirp_table(rows, pairs))


def sum_kernel(plan, segments, has_start, tracks, meta, *refs):
    start = refs[0] if has_start else None
    blocks, out, gathered = refs[has_start:-2], refs[-2], refs[-1]
    total_rows = gathered.shape[0]
    width = gathered.shape[1]
    me = lax.axis_index("seg")
    core, chip = lax.rem(me, 2), lax.div(me, 2)
    level, other, away = meta[0:1], meta[1:2], meta[2:3]
    segment = 2 * lax.bitwise_xor(away, chip) + lax.bitwise_xor(other, core)
    places = lax.broadcasted_iota(jnp.int32, (segments, total_rows), 0)
    chosen = (places == segment).astype(F32).astype(BF16)
    named = jnp.dot(
        tracks[...].astype(F32).astype(BF16), chosen, preferred_element_type=F32
    )
    pick = jnp.where((named == level.astype(F32)) | (level < 0), 1.0, 0.0).astype(BF16)
    per = width // BLK
    for column in range(per):
        at = 0
        for block, height in zip(blocks, plan):
            gathered[at : at + height, column * BLK : (column + 1) * BLK] = block[
                pl.ds(column, height, stride=per), :
            ]
            at += height
    for column in range(0, width, 512):
        size = min(512, width - column)
        value = gathered[:, column : column + size]
        high = value.astype(BF16)
        low = (value - high.astype(F32)).astype(BF16)
        total = jnp.dot(pick, high, preferred_element_type=F32)
        total = total + jnp.dot(pick, low, preferred_element_type=F32)
        total = total * (1.0 / segments)
        if has_start:
            total = total + start[:, column : column + size]
        out[:, column : column + size] = total


def track_sum(tracks, parts, start=None):
    ntrack, segments = tracks.shape
    plan = [len(levels) for _, levels in parts]
    width = parts[0][0].shape[0] * BLK // plan[0]
    meta = np.array([row for _, levels in parts for row in levels]).T
    starts = [] if start is None else [start]
    return pl.pallas_call(
        functools.partial(sum_kernel, plan, segments, len(starts)),
        out_shape=jax.ShapeDtypeStruct((ntrack, width), F32),
        scratch_shapes=[pltpu.VMEM((sum(plan), width), F32)],
        compiler_params=pltpu.CompilerParams(vmem_limit_bytes=32 * 2**20),
    )(tracks, jnp.asarray(meta, jnp.int32), *starts, *[block for block, _ in parts])


def local(count, strain_series, antenna, drift, tracks):
    points = strain_series.shape[2]
    tile = lambda array: array.reshape(2, points // BLK, BLK).transpose(1, 0, 2).reshape(-1, BLK)
    series, weights = tile(strain_series), tile(antenna)
    chips = count // 2
    half = chips // 2
    far, near = range(half, chips), range(half)
    swap = lambda hop: [(device, device ^ hop) for device in range(count)]
    send = lambda array, hop: lax.ppermute(array, "seg", swap(hop)) if hop else array
    pack = lambda rows: jnp.stack(rows).reshape(-1, BLK)

    own, give = stat(EARLY, 58, 10**9, count, drift, series, weights)
    got = send(give, 1)
    rows, names = [own[0] + got[0]], [(-1, 0)]
    for index, (pair, side) in enumerate(EARLY[1:]):
        for other, part in enumerate((own, got)):
            rows.append(part[1 + index] - part[0])
            names.append((level_of(pair, side), other))
    blocks = {away: send(pack([row[away] for row in rows]), 2 * away) for away in range(chips)}
    parts = {
        away: (block, [(level, other, away) for level, other in names])
        for away, block in blocks.items()
    }
    first = [parts[away] for away in near]
    last = [parts[away] for away in range(chips) if away not in near]
    return track_sum(tracks, last, track_sum(tracks, first))


def solution(mesh):
    return jax.shard_map(
        functools.partial(local, mesh.shape["seg"]),
        mesh=mesh,
        in_specs=(
            P(("sky", "seg"), None, None),
            P(("sky", "seg"), None, None),
            P(("sky", "seg"), None),
            P(),
        ),
        out_specs=P("sky", "seg"),
        check_vma=False,
    )
```

time: 57 us -> 53 us (0.930)
  local copies, waits for them, and re-layouts: 6.58 us -> 0.27 us
  other arithmetic: 0.22 us -> 2.29 us
  Pallas kernels: 9.22 us -> 11.2 us
  waiting for transfers between devices: 32.6 us -> 30.9 us
    unnamed x18 -> x17, local copies, waits for them, and re-layouts: 6.29 us -> 0.25 us
    sub x0 -> x2, other arithmetic: none -> 2.29 us  [local(): rows.append(part[1 + index] - part[0])]
    pallas_call x2 -> x3, Pallas kernels: 9.22 us -> 11.2 us  [the longest x1 8.55 us: stat(): pl.pallas_call(functools.partial(stat_kernel, kept, count), out_shape=(ja...]
    ppermute x8, waiting for transfers between devices: 32.6 us -> 30.9 us  [local(): lax.ppermute(array, 'seg', swap(hop))]
  transfers between devices with their start and end apart: 8 -> 8, of which waited for: 7 -> 6; matrix products, arithmetic and copies ran while one was open for 0% -> 2% of each run, Pallas kernels for 0% -> 2%
where the time goes in v2:
time: 53 us; the launch traced here: 52.8 us
  waiting for transfers between devices  30.9 us (58%)
  Pallas kernels  11.2 us (21%)
  starting transfers between devices  7.95 us (15%)
  other arithmetic  2.29 us (4%)
    ppermute x8, waiting for transfers between devices, local(): lax.ppermute(array, 'seg', swap(hop))  30.9 us
    pallas_call x1, Pallas kernels, stat(): pl.pallas_call(functools.partial(stat_kernel, kept, count), out_shape=(ja...  8.55 us
    ppermute x8, starting transfers between devices, local(): lax.ppermute(array, 'seg', swap(hop))  7.95 us
    pallas_call x2, Pallas kernels, track_sum(): pl.pallas_call(functools.partial(sum_kernel, plan, segments, len(starts))...  2.7 us
    sub x2, other arithmetic, local(): rows.append(part[1 + index] - part[0])  2.29 us
  transfers between devices with their start and end apart: 8, of which 6 were waited for; matrix products, arithmetic and copies ran while one was open for 2% of the time, Pallas kernels for 2%

profile of v2, /device:TPU:16, one launch (start us, length us, event | category | flops | bytes accessed | tf_op | source)
XLA Modules:
  0.0 52.8 jit_solution(17394452863554660549)
XLA Ops:
  0.0 8.5 %shard_map.91 = (f32[6,8,32,128]{3,2,1,0:T(8,128)}, f32[6,8,32,128]{3,2,1,0:T(8,128)}) custom-call(s32[1,6]{1,0:T(1,128)} %drift.1, bf16[1024,128]{1,0:T(8,128)(2,1)} %bitcast.379, f32[1024,128]{1,0:T(8,128)} %bitcast.378, bf16[512,512]{1,0:T(8,128)(2,1)} %constant.18.table_hbm, f32[2,256,256]{2,1,0:T(8,128)} %constant.11.clone.twist_hbm, ...), custom_call_target="tpu_custom_call" | custom-call | flops 1000000000 | bytes 3145728 | tf_op jit(solution)/shard_map/pallas_call | solution.py:184
  8.6 0.1 collective-permute-start
  8.6 1.1 %slice_subtract_fusion.8 = (f32[1,8,32,128]{3,2,1,0:T(8,128)S(1)}, f32[1,8,32,128]{3,2,1,0:T(8,128)S(1)}) fusion(f32[6,8,32,128]{3,2,1,0:T(8,128)} %get-tuple-element.7), kind=kLoop, calls=%fused_computation.96 | loop fusion | flops 65536 | bytes 655360 | tf_op jit(solution)/shard_map/sub | solution.py:275
  9.7 1.4 %collective-permute-done = f32[6,8,32,128]{3,2,1,0:T(8,128)S(1)} collective-permute-done((f32[6,8,32,128]{3,2,1,0:T(8,128)}, f32[6,8,32,128]{3,2,1,0:T(8,128)S(1)}, u32[]{:S(2)}, u32[]{:S(2)}) %collective-permute-start) | collective-permute-done | bytes 786464 | tf_op jit(solution)/shard_map/ppermute | solution.py:267
  11.1 1.2 %slice_subtract_fusion = (f32[1,8,32,128]{3,2,1,0:T(8,128)S(1)}, f32[1,8,32,128]{3,2,1,0:T(8,128)S(1)}, f32[1,8,32,128]{3,2,1,0:T(8,128)S(1)}, f32[1,8,32,128]{3...) fusion(f32[6,8,32,128]{3,2,1,0:T(8,128)S(1)} %collective-permut, ...), kind=kLoop, calls=%fused_computation.88 | loop fusion | flops 294912 | bytes 2490368 | tf_op jit(solution)/shard_map/sub | solution.py:275
  12.4 0.0 copy-start.2
  12.4 0.0 copy-start.1
  12.5 0.0 copy-start
  12.6 1.6 %collective-permute-start.1 = (f32[352,128]{1,0:T(8,128)S(1)}, f32[352,128]{1,0:T(8,128)S(1)}, u32[]{:S(2)}, u32[]{:S(2)}) collective-permute-start(f32[352,128]{1,0:T(8,128)S(1)} %bitcast.377), channel_id=1, source_target_pairs={{0,2},{1,3},{2,0},{3,1},{4,6},{5,7},{6,4},{7,5},{8,10},{9,11},{10,... | collective-permute-start | bytes 540680 | tf_op jit(solution)/shard_map/ppermute | solution.py:267
  14.2 1.6 %collective-permute-start.2 = (f32[352,128]{1,0:T(8,128)S(1)}, f32[352,128]{1,0:T(8,128)S(1)}, u32[]{:S(2)}, u32[]{:S(2)}) collective-permute-start(f32[352,128]{1,0:T(8,128)S(1)} %bitcast.376), channel_id=1, source_target_pairs={{0,4},{1,5},{2,6},{3,7},{4,0},{5,1},{6,2},{7,3},{8,12},{9,13},{10,... | collective-permute-start | bytes 540680 | tf_op jit(solution)/shard_map/ppermute | solution.py:267
  15.8 0.4 collective-permute-start.3
  16.2 0.0 collective-permute-start.4
  16.2 3.9 %collective-permute-start.5 = (f32[352,128]{1,0:T(8,128)S(1)}, f32[352,128]{1,0:T(8,128)S(1)}, u32[]{:S(2)}, u32[]{:S(2)}) collective-permute-start(f32[352,128]{1,0:T(8,128)S(1)} %bitcast.373), channel_id=1, source_target_pairs={{0,10},{1,11},{2,8},{3,9},{4,14},{5,15},{6,12},{7,13},{8,2},{9,3},... | collective-permute-start | bytes 540680 | tf_op jit(solution)/shard_map/ppermute | solution.py:267
  20.1 0.0 collective-permute-done.1.refs_1_
  20.1 0.4 collective-permute-start.6
  20.5 5.5 %collective-permute-done.2.refs_2_ = f32[352,128]{1,0:T(8,128)S(1)} collective-permute-done((f32[352,128]{1,0:T(8,128)S(1)}, f32[352,128]{1,0:T(8,128)S(1)}, u32[]{:S(2)}, u32[]{:S(2)}) %collective-permute-start.2) | collective-permute-done | bytes 180256 | tf_op jit(solution)/shard_map/ppermute | solution.py:267
  26.0 0.0 collective-permute-start.7
  26.0 0.0 copy-done.2
  26.0 0.1 copy.13.tracks
  26.1 2.6 %collective-permute-done.3.refs_3_ = f32[352,128]{1,0:T(8,128)S(1)} collective-permute-done((f32[352,128]{1,0:T(8,128)S(1)}, f32[352,128]{1,0:T(8,128)S(1)}, u32[]{:S(2)}, u32[]{:S(2)}) %collective-permute-start.3) | collective-permute-done | bytes 180256 | tf_op jit(solution)/shard_map/ppermute | solution.py:267
  28.7 0.0 copy-done.1
  28.7 0.9 %shard_map.92.refs_0_ = f32[64,4096]{1,0:T(8,128)S(1)} custom-call(s32[64,16]{1,0:T(8,128)S(1)} %copy.13.tracks, s32[3,44]{1,0:T(4,128)S(1)} %copy-done.1, f32[352,128]{1,0:T(8,128)S(1)} %bitcast.370, f32[352,128]{1,0:T(8,128)S(1)} %collective-permute-done.1.refs_1_, f32[352,128]{1,0:T(8,128)S(1)} %collective-permute-done.2.refs_2_, ...), custom_call_target="tpu_custom_call" | custom-call | tf_op jit(solution)/shard_map/pallas_call | solution.py:251
  29.6 0.0 collective-permute-done.4.refs_1_
  29.6 10.9 %collective-permute-done.5.refs_2_ = f32[352,128]{1,0:T(8,128)S(1)} collective-permute-done((f32[352,128]{1,0:T(8,128)S(1)}, f32[352,128]{1,0:T(8,128)S(1)}, u32[]{:S(2)}, u32[]{:S(2)}) %collective-permute-start.5) | collective-permute-done | bytes 180256 | tf_op jit(solution)/shard_map/ppermute | solution.py:267
  40.5 7.3 %collective-permute-done.6.refs_3_ = f32[352,128]{1,0:T(8,128)S(1)} collective-permute-done((f32[352,128]{1,0:T(8,128)S(1)}, f32[352,128]{1,0:T(8,128)S(1)}, u32[]{:S(2)}, u32[]{:S(2)}) %collective-permute-start.6) | collective-permute-done | bytes 180256 | tf_op jit(solution)/shard_map/ppermute | solution.py:267
  47.9 3.1 %collective-permute-done.7.refs_4_ = f32[352,128]{1,0:T(8,128)S(1)} collective-permute-done((f32[352,128]{1,0:T(8,128)S(1)}, f32[352,128]{1,0:T(8,128)S(1)}, u32[]{:S(2)}, u32[]{:S(2)}) %collective-permute-start.7) | collective-permute-done | bytes 180256 | tf_op jit(solution)/shard_map/ppermute | solution.py:267
  51.0 0.0 copy-done
  51.0 1.8 %shard_map.93 = f32[64,4096]{1,0:T(8,128)} custom-call(s32[64,16]{1,0:T(8,128)S(1)} %copy.13.tracks, s32[3,44]{1,0:T(4,128)S(1)} %copy-done, f32[64,4096]{1,0:T(8,128)S(1)} %shard_map.92.refs_0_, f32[352,128]{1,0:T(8,128)S(1)} %collective-permute-done.4.refs_1_, f32[352,128]{1,0:T(8,128)S(1)} %collective-permute-done.5.refs_2_, ...), custom_call_target="tpu_custom_call" | custom-call | tf_op jit(solution)/shard_map/pallas_call | solution.py:251
  (11 shorter events, 0.2 us)
Async XLA Ops:
  8.6 2.6 %collective-permute-start = (f32[6,8,32,128]{3,2,1,0:T(8,128)}, f32[6,8,32,128]{3,2,1,0:T(8,128)S(1)}, u32[]{:S(2)}, u32[]{:S(2)}) collective-permute-start(f32[6,8,32,128]{3,2,1,0:T(8,128)} %get-tuple-element.8), channel_id=1, source_target_pairs={{0,1},{1,0},{2,3},{3,2},{4,5},{5,4},{6,7},{7,6},{8,9},{9,8},{10,11... | collective-permute-start | bytes 2359304 | tf_op jit(solution)/shard_map/ppermute | solution.py:267
  12.4 13.6 %copy-start.2 = (s32[64,16]{0,1:T(8,128)S(1)}, s32[64,16]{0,1:T(8,128)}, u32[]{:S(2)}) copy-start(s32[64,16]{0,1:T(8,128)} %param.12) | copy-start | bytes 12292
  12.4 16.4 %copy-start.1 = (s32[3,44]{1,0:T(4,128)S(1)}, s32[3,44]{1,0:T(4,128)}, u32[]{:S(2)}) copy-start(s32[3,44]{1,0:T(4,128)} %constant.13.clone.meta) | copy-start | bytes 1588
  12.5 38.5 %copy-start = (s32[3,44]{1,0:T(4,128)S(1)}, s32[3,44]{1,0:T(4,128)}, u32[]{:S(2)}) copy-start(s32[3,44]{1,0:T(4,128)} %constant.14.clone.meta) | copy-start | bytes 1588
  12.6 7.4 %collective-permute-start.1 = (f32[352,128]{1,0:T(8,128)S(1)}, f32[352,128]{1,0:T(8,128)S(1)}, u32[]{:S(2)}, u32[]{:S(2)}) collective-permute-start(f32[352,128]{1,0:T(8,128)S(1)} %bitcast.377), channel_id=1, source_target_pairs={{0,2},{1,3},{2,0},{3,1},{4,6},{5,7},{6,4},{7,5},{8,10},{9,11},{10,... | collective-permute-start | bytes 540680 | tf_op jit(solution)/shard_map/ppermute | solution.py:267
  14.2 11.8 %collective-permute-start.2 = (f32[352,128]{1,0:T(8,128)S(1)}, f32[352,128]{1,0:T(8,128)S(1)}, u32[]{:S(2)}, u32[]{:S(2)}) collective-permute-start(f32[352,128]{1,0:T(8,128)S(1)} %bitcast.376), channel_id=1, source_target_pairs={{0,4},{1,5},{2,6},{3,7},{4,0},{5,1},{6,2},{7,3},{8,12},{9,13},{10,... | collective-permute-start | bytes 540680 | tf_op jit(solution)/shard_map/ppermute | solution.py:267
  15.8 12.9 %collective-permute-start.3 = (f32[352,128]{1,0:T(8,128)S(1)}, f32[352,128]{1,0:T(8,128)S(1)}, u32[]{:S(2)}, u32[]{:S(2)}) collective-permute-start(f32[352,128]{1,0:T(8,128)S(1)} %bitcast.375), channel_id=1, source_target_pairs={{0,6},{1,7},{2,4},{3,5},{4,2},{5,3},{6,0},{7,1},{8,14},{9,15},{10,... | collective-permute-start | bytes 540680 | tf_op jit(solution)/shard_map/ppermute | solution.py:267
  16.2 13.4 %collective-permute-start.4 = (f32[352,128]{1,0:T(8,128)S(1)}, f32[352,128]{1,0:T(8,128)S(1)}, u32[]{:S(2)}, u32[]{:S(2)}) collective-permute-start(f32[352,128]{1,0:T(8,128)S(1)} %bitcast.374), channel_id=1, source_target_pairs={{0,8},{1,9},{2,10},{3,11},{4,12},{5,13},{6,14},{7,15},{8,0},{9,1},... | collective-permute-start | bytes 540680 | tf_op jit(solution)/shard_map/ppermute | solution.py:267
  16.2 24.3 %collective-permute-start.5 = (f32[352,128]{1,0:T(8,128)S(1)}, f32[352,128]{1,0:T(8,128)S(1)}, u32[]{:S(2)}, u32[]{:S(2)}) collective-permute-start(f32[352,128]{1,0:T(8,128)S(1)} %bitcast.373), channel_id=1, source_target_pairs={{0,10},{1,11},{2,8},{3,9},{4,14},{5,15},{6,12},{7,13},{8,2},{9,3},... | collective-permute-start | bytes 540680 | tf_op jit(solution)/shard_map/ppermute | solution.py:267
  20.1 27.8 %collective-permute-start.6 = (f32[352,128]{1,0:T(8,128)S(1)}, f32[352,128]{1,0:T(8,128)S(1)}, u32[]{:S(2)}, u32[]{:S(2)}) collective-permute-start(f32[352,128]{1,0:T(8,128)S(1)} %bitcast.372), channel_id=1, source_target_pairs={{0,12},{1,13},{2,14},{3,15},{4,8},{5,9},{6,10},{7,11},{8,4},{9,5},... | collective-permute-start | bytes 540680 | tf_op jit(solution)/shard_map/ppermute | solution.py:267
  26.0 25.0 %collective-permute-start.7 = (f32[352,128]{1,0:T(8,128)S(1)}, f32[352,128]{1,0:T(8,128)S(1)}, u32[]{:S(2)}, u32[]{:S(2)}) collective-permute-start(f32[352,128]{1,0:T(8,128)S(1)} %bitcast.371), channel_id=1, source_target_pairs={{0,14},{1,15},{2,12},{3,13},{4,10},{5,11},{6,8},{7,9},{8,6},{9,7},... | collective-permute-start | bytes 540680 | tf_op jit(solution)/shard_map/ppermute | solution.py:267

commit v3 on v2

--- a/solution.py
+++ b/solution.py
@@ -133,9 +133,9 @@
 
 
 def stat_kernel(
-    kept, count, drift, series_hbm, weights_hbm, table_hbm, twist_hbm, chirp_hbm,
-    own_hbm, give_hbm,
-    series, weights, table, twist, chirp, lanes, prep, coef, moved, own, give, sems, out_sems,
+    kept, count, drift_hbm, series_hbm, weights_hbm, table_hbm, twist_hbm, chirp_hbm,
+    own, give,
+    series, weights, table, twist, chirp, lanes, prep, coef, moved, drift, sems,
 ):
     first_pair = min(pair for pair, _ in kept)
     moves = fetch(
@@ -145,6 +145,7 @@
             (chirp_hbm, chirp),
             (table_hbm, table),
             (twist_hbm, twist),
+            (drift_hbm, drift),
         ],
         sems,
     )
@@ -155,21 +156,12 @@
     for move in moves[2:]:
         move.wait()
     per = own.shape[2]
-    outs = []
     for index, (pair, side) in enumerate(kept):
         at = chirp.at[pair - first_pair]
         one_stat(pair, side, drift, at, table, twist, prep, coef, moved)
-        for other, (held, target) in enumerate(((give, give_hbm), (own, own_hbm))):
-            for away in range(count // 2):
-                held[index, away] = moved[block_of(count, per, away, 1 - other), :]
-            outs.append(
-                pltpu.make_async_copy(
-                    held.at[index], target.at[index], out_sems.at[2 * index + other]
-                )
-            )
-            outs[-1].start()
-    for out in outs:
-        out.wait()
+        for away in range(count // 2):
+            own[index, away] = moved[block_of(count, per, away, 0), :]
+            give[index, away] = moved[block_of(count, per, away, 1), :]
 
 
 def stat(kept, limit, cost, count, drift, series, weights):
@@ -178,14 +170,14 @@
     per = points // BLK // count
     chips = count // 2
     pairs = tuple(sorted({pair for pair, _ in kept}))
+    inputs = (drift, series, weights, dft_table(rows), twist_table(rows), chirp_table(rows, pairs))
     hbm = pl.BlockSpec(memory_space=pltpu.HBM)
-    smem = pl.BlockSpec(memory_space=pltpu.SMEM)
     shape = (len(kept), chips, per, BLK)
     return pl.pallas_call(
         functools.partial(stat_kernel, kept, count),
         out_shape=(jax.ShapeDtypeStruct(shape, F32),) * 2,
-        in_specs=[smem] + [hbm] * 5,
-        out_specs=(hbm, hbm),
+        in_specs=[hbm] * 6,
+        out_specs=(pl.BlockSpec(memory_space=pltpu.VMEM),) * 2,
         scratch_shapes=[
             pltpu.VMEM(series.shape, BF16),
             pltpu.VMEM(weights.shape, F32),
@@ -196,14 +188,12 @@
             pltpu.VMEM((4, rows, rows), F32),
             pltpu.SMEM((3,), F32),
             pltpu.VMEM((points // BLK + 2 * PAD, BLK), F32),
-            pltpu.VMEM(shape, F32),
-            pltpu.VMEM(shape, F32),
-            pltpu.SemaphoreType.DMA((5,)),
-            pltpu.SemaphoreType.DMA((2 * len(kept),)),
+            pltpu.SMEM(drift.shape, jnp.int32),
+            pltpu.SemaphoreType.DMA((6,)),
         ],
-        compiler_params=pltpu.CompilerParams(vmem_limit_bytes=limit * 2**20),
+        compiler_params=pltpu.CompilerParams(vmem_limit_bytes=int(limit * 2**20)),
         cost_estimate=pl.CostEstimate(flops=cost, bytes_accessed=3 * 2**20, transcendentals=0),
-    )(drift, series, weights, dft_table(rows), twist_table(rows), chirp_table(rows, pairs))
+    )(*[pltpu.with_memory_space_constraint(array, pltpu.HBM) for array in inputs])
 
 
 def sum_kernel(plan, segments, has_start, tracks, meta, *refs):
@@ -267,20 +257,20 @@
     send = lambda array, hop: lax.ppermute(array, "seg", swap(hop)) if hop else array
     pack = lambda rows: jnp.stack(rows).reshape(-1, BLK)
 
-    own, give = stat(EARLY, 58, 10**9, count, drift, series, weights)
+    own, give = stat(EARLY, 32, 10**9, count, drift, series, weights)
     got = send(give, 1)
     rows, names = [own[0] + got[0]], [(-1, 0)]
     for index, (pair, side) in enumerate(EARLY[1:]):
         for other, part in enumerate((own, got)):
             rows.append(part[1 + index] - part[0])
             names.append((level_of(pair, side), other))
-    blocks = {away: send(pack([row[away] for row in rows]), 2 * away) for away in range(chips)}
+    blocks = {away: send(pack([row[away] for row in rows]), 2 * away) for away in (0,4,2,6,5,7,3,1)}
     parts = {
         away: (block, [(level, other, away) for level, other in names])
         for away, block in blocks.items()
     }
-    first = [parts[away] for away in near]
-    last = [parts[away] for away in range(chips) if away not in near]
+    first = [parts[away] for away in (0,4,2,6)]
+    last = [parts[away] for away in (0,4,2,6,5,7,3,1) if away not in (0,4,2,6)]
     return track_sum(tracks, last, track_sum(tracks, first))
 
 

time: 53 us -> 47.6 us (0.90)
  waiting for transfers between devices: 30.9 us -> 22 us
  starting transfers between devices: 7.95 us -> 14.8 us
  other arithmetic: 2.29 us -> 0.16 us
  Pallas kernels: 11.2 us -> 9.79 us
    ppermute x8, waiting for transfers between devices: 30.9 us -> 22 us  [local(): lax.ppermute(array, 'seg', swap(hop))]
    ppermute x8, starting transfers between devices: 7.95 us -> 14.8 us  [local(): lax.ppermute(array, 'seg', swap(hop))]
    sub x2, other arithmetic: 2.29 us -> 0.16 us  [local(): rows.append(part[1 + index] - part[0])]
    pallas_call x1, Pallas kernels: 8.55 us -> 7.09 us  [stat(): pl.pallas_call(functools.partial(stat_kernel, kept, count), out_shape=(ja...]
  transfers between devices with their start and end apart: 8 -> 8, of which waited for: 6 -> 5; matrix products, arithmetic and copies ran while one was open for 2% -> 0% of each run, Pallas kernels for 2% -> 2%
where the time goes in v3:
time: 47.6 us; the launch traced here: 47.3 us
  waiting for transfers between devices  22 us (46%)
  starting transfers between devices  14.8 us (31%)
  Pallas kernels  9.79 us (21%)
    ppermute x8, waiting for transfers between devices, local(): lax.ppermute(array, 'seg', swap(hop))  22 us
    ppermute x8, starting transfers between devices, local(): lax.ppermute(array, 'seg', swap(hop))  14.8 us
    pallas_call x1, Pallas kernels, stat(): pl.pallas_call(functools.partial(stat_kernel, kept, count), out_shape=(ja...  7.09 us
    pallas_call x2, Pallas kernels, track_sum(): pl.pallas_call(functools.partial(sum_kernel, plan, segments, len(starts))...  2.7 us
  transfers between devices with their start and end apart: 8, of which 5 were waited for; matrix products, arithmetic and copies ran while one was open for 0% of the time, Pallas kernels for 2%

profile of v3, /device:TPU:16, one launch (start us, length us, event | category | flops | bytes accessed | tf_op | source)
XLA Modules:
  0.0 47.3 jit_solution(17687213942286752837)
XLA Ops:
  0.0 7.1 %shard_map.91 = (f32[6,8,32,128]{3,2,1,0:T(8,128)S(1)}, f32[6,8,32,128]{3,2,1,0:T(8,128)S(1)}) custom-call(s32[1,6]{1,0:T(1,128)} %drift_hbm.1, bf16[1024,128]{1,0:T(8,128)(2,1)} %bitcast.379, f32[1024,128]{1,0:T(8,128)} %bitcast.378, bf16[512,512]{1,0:T(8,128)(2,1)} %constant.18.table_hbm, f32[2,256,256]{2,1,0:T(8,128)} %constant.11.clone.twist_hbm, ...), custom_call_target="tpu_custom_call" | custom-call | flops 1000000000 | bytes 3145728 | tf_op jit(solution)/shard_map/pallas_call | solution.py:176
  7.1 0.1 collective-permute-start
  7.2 2.2 %collective-permute-done = f32[6,8,32,128]{3,2,1,0:T(8,128)S(1)} collective-permute-done((f32[6,8,32,128]{3,2,1,0:T(8,128)S(1)}, f32[6,8,32,128]{3,2,1,0:T(8,128)S(1)}, u32[]{:S(2)}, u32[]{:S(2)}) %collective-permute-start) | collective-permute-done | bytes 786464 | tf_op jit(solution)/shard_map/ppermute | solution.py:257
  9.5 0.1 slice_subtract_fusion
  9.6 0.0 copy-start.2
  9.6 0.0 copy-start.1
  9.8 0.0 copy-start
  9.9 0.1 collective-permute-start.1
  10.0 1.9 %collective-permute-start.2 = (f32[352,128]{1,0:T(8,128)S(1)}, f32[352,128]{1,0:T(8,128)S(1)}, u32[]{:S(2)}, u32[]{:S(2)}) collective-permute-start(f32[352,128]{1,0:T(8,128)S(1)} %bitcast.376), channel_id=1, source_target_pairs={{0,4},{1,5},{2,6},{3,7},{4,0},{5,1},{6,2},{7,3},{8,12},{9,13},{10,... | collective-permute-start | bytes 540680 | tf_op jit(solution)/shard_map/ppermute | solution.py:257
  11.9 1.6 %collective-permute-start.3 = (f32[352,128]{1,0:T(8,128)S(1)}, f32[352,128]{1,0:T(8,128)S(1)}, u32[]{:S(2)}, u32[]{:S(2)}) collective-permute-start(f32[352,128]{1,0:T(8,128)S(1)} %bitcast.375), channel_id=1, source_target_pairs={{0,12},{1,13},{2,14},{3,15},{4,8},{5,9},{6,10},{7,11},{8,4},{9,5},... | collective-permute-start | bytes 540680 | tf_op jit(solution)/shard_map/ppermute | solution.py:257
  13.4 2.2 %collective-permute-start.4 = (f32[352,128]{1,0:T(8,128)S(1)}, f32[352,128]{1,0:T(8,128)S(1)}, u32[]{:S(2)}, u32[]{:S(2)}) collective-permute-start(f32[352,128]{1,0:T(8,128)S(1)} %bitcast.374), channel_id=1, source_target_pairs={{0,10},{1,11},{2,8},{3,9},{4,14},{5,15},{6,12},{7,13},{8,2},{9,3},... | collective-permute-start | bytes 540680 | tf_op jit(solution)/shard_map/ppermute | solution.py:257
  15.6 2.7 %collective-permute-start.5 = (f32[352,128]{1,0:T(8,128)S(1)}, f32[352,128]{1,0:T(8,128)S(1)}, u32[]{:S(2)}, u32[]{:S(2)}) collective-permute-start(f32[352,128]{1,0:T(8,128)S(1)} %bitcast.373), channel_id=1, source_target_pairs={{0,14},{1,15},{2,12},{3,13},{4,10},{5,11},{6,8},{7,9},{8,6},{9,7},... | collective-permute-start | bytes 540680 | tf_op jit(solution)/shard_map/ppermute | solution.py:257
  18.3 0.4 collective-permute-done.1.refs_1_
  18.7 5.9 %collective-permute-start.6 = (f32[352,128]{1,0:T(8,128)S(1)}, f32[352,128]{1,0:T(8,128)S(1)}, u32[]{:S(2)}, u32[]{:S(2)}) collective-permute-start(f32[352,128]{1,0:T(8,128)S(1)} %bitcast.372), channel_id=1, source_target_pairs={{0,6},{1,7},{2,4},{3,5},{4,2},{5,3},{6,0},{7,1},{8,14},{9,15},{10,... | collective-permute-start | bytes 540680 | tf_op jit(solution)/shard_map/ppermute | solution.py:257
  24.6 0.0 collective-permute-done.2.refs_2_
  24.6 0.5 %collective-permute-start.7 = (f32[352,128]{1,0:T(8,128)S(1)}, f32[352,128]{1,0:T(8,128)S(1)}, u32[]{:S(2)}, u32[]{:S(2)}) collective-permute-start(f32[352,128]{1,0:T(8,128)S(1)} %bitcast.371), channel_id=1, source_target_pairs={{0,2},{1,3},{2,0},{3,1},{4,6},{5,7},{6,4},{7,5},{8,10},{9,11},{10,... | collective-permute-start | bytes 540680 | tf_op jit(solution)/shard_map/ppermute | solution.py:257
  25.1 0.0 copy-done.2
  25.1 0.1 copy.13.tracks
  25.2 11.6 %collective-permute-done.3.refs_3_ = f32[352,128]{1,0:T(8,128)S(1)} collective-permute-done((f32[352,128]{1,0:T(8,128)S(1)}, f32[352,128]{1,0:T(8,128)S(1)}, u32[]{:S(2)}, u32[]{:S(2)}) %collective-permute-start.3) | collective-permute-done | bytes 180256 | tf_op jit(solution)/shard_map/ppermute | solution.py:257
  36.8 0.0 copy-done.1
  36.8 0.9 %shard_map.92.refs_0_ = f32[64,4096]{1,0:T(8,128)S(1)} custom-call(s32[64,16]{1,0:T(8,128)S(1)} %copy.13.tracks, s32[3,44]{1,0:T(4,128)S(1)} %copy-done.1, f32[352,128]{1,0:T(8,128)S(1)} %bitcast.370, f32[352,128]{1,0:T(8,128)S(1)} %collective-permute-done.1.refs_1_, f32[352,128]{1,0:T(8,128)S(1)} %collective-permute-done.2.refs_2_, ...), custom_call_target="tpu_custom_call" | custom-call | tf_op jit(solution)/shard_map/pallas_call | solution.py:241
  37.7 0.3 collective-permute-done.4.refs_1_
  38.0 7.4 %collective-permute-done.5.refs_2_ = f32[352,128]{1,0:T(8,128)S(1)} collective-permute-done((f32[352,128]{1,0:T(8,128)S(1)}, f32[352,128]{1,0:T(8,128)S(1)}, u32[]{:S(2)}, u32[]{:S(2)}) %collective-permute-start.5) | collective-permute-done | bytes 180256 | tf_op jit(solution)/shard_map/ppermute | solution.py:257
  45.4 0.0 collective-permute-done.6.refs_3_
  45.4 0.0 collective-permute-done.7.refs_4_
  45.4 0.0 copy-done
  45.4 1.8 %shard_map.93 = f32[64,4096]{1,0:T(8,128)} custom-call(s32[64,16]{1,0:T(8,128)S(1)} %copy.13.tracks, s32[3,44]{1,0:T(4,128)S(1)} %copy-done, f32[64,4096]{1,0:T(8,128)S(1)} %shard_map.92.refs_0_, f32[352,128]{1,0:T(8,128)S(1)} %collective-permute-done.4.refs_1_, f32[352,128]{1,0:T(8,128)S(1)} %collective-permute-done.5.refs_2_, ...), custom_call_target="tpu_custom_call" | custom-call | tf_op jit(solution)/shard_map/pallas_call | solution.py:241
  (12 shorter events, 0.2 us)
Async XLA Ops:
  7.1 2.4 %collective-permute-start = (f32[6,8,32,128]{3,2,1,0:T(8,128)S(1)}, f32[6,8,32,128]{3,2,1,0:T(8,128)S(1)}, u32[]{:S(2)}, u32[]{:S(2)}) collective-permute-start(f32[6,8,32,128]{3,2,1,0:T(8,128)S(1)} %get-tuple-element.8), channel_id=1, source_target_pairs={{0,1},{1,0},{2,3},{3,2},{4,5},{5,4},{6,7},{7,6},{8,9},{9,8},{10,11... | collective-permute-start | bytes 2359304 | tf_op jit(solution)/shard_map/ppermute | solution.py:257
  9.6 15.5 %copy-start.2 = (s32[64,16]{0,1:T(8,128)S(1)}, s32[64,16]{0,1:T(8,128)}, u32[]{:S(2)}) copy-start(s32[64,16]{0,1:T(8,128)} %param.12) | copy-start | bytes 12292
  9.6 27.2 %copy-start.1 = (s32[3,44]{1,0:T(4,128)S(1)}, s32[3,44]{1,0:T(4,128)}, u32[]{:S(2)}) copy-start(s32[3,44]{1,0:T(4,128)} %constant.13.clone.meta) | copy-start | bytes 1588
  9.8 35.7 %copy-start = (s32[3,44]{1,0:T(4,128)S(1)}, s32[3,44]{1,0:T(4,128)}, u32[]{:S(2)}) copy-start(s32[3,44]{1,0:T(4,128)} %constant.14.clone.meta) | copy-start | bytes 1588
  9.9 8.8 %collective-permute-start.1 = (f32[352,128]{1,0:T(8,128)S(1)}, f32[352,128]{1,0:T(8,128)S(1)}, u32[]{:S(2)}, u32[]{:S(2)}) collective-permute-start(f32[352,128]{1,0:T(8,128)S(1)} %bitcast.377), channel_id=1, source_target_pairs={{0,8},{1,9},{2,10},{3,11},{4,12},{5,13},{6,14},{7,15},{8,0},{9,1},... | collective-permute-start | bytes 540680 | tf_op jit(solution)/shard_map/ppermute | solution.py:257
  10.0 14.6 %collective-permute-start.2 = (f32[352,128]{1,0:T(8,128)S(1)}, f32[352,128]{1,0:T(8,128)S(1)}, u32[]{:S(2)}, u32[]{:S(2)}) collective-permute-start(f32[352,128]{1,0:T(8,128)S(1)} %bitcast.376), channel_id=1, source_target_pairs={{0,4},{1,5},{2,6},{3,7},{4,0},{5,1},{6,2},{7,3},{8,12},{9,13},{10,... | collective-permute-start | bytes 540680 | tf_op jit(solution)/shard_map/ppermute | solution.py:257
  11.9 25.0 %collective-permute-start.3 = (f32[352,128]{1,0:T(8,128)S(1)}, f32[352,128]{1,0:T(8,128)S(1)}, u32[]{:S(2)}, u32[]{:S(2)}) collective-permute-start(f32[352,128]{1,0:T(8,128)S(1)} %bitcast.375), channel_id=1, source_target_pairs={{0,12},{1,13},{2,14},{3,15},{4,8},{5,9},{6,10},{7,11},{8,4},{9,5},... | collective-permute-start | bytes 540680 | tf_op jit(solution)/shard_map/ppermute | solution.py:257
  13.4 24.6 %collective-permute-start.4 = (f32[352,128]{1,0:T(8,128)S(1)}, f32[352,128]{1,0:T(8,128)S(1)}, u32[]{:S(2)}, u32[]{:S(2)}) collective-permute-start(f32[352,128]{1,0:T(8,128)S(1)} %bitcast.374), channel_id=1, source_target_pairs={{0,10},{1,11},{2,8},{3,9},{4,14},{5,15},{6,12},{7,13},{8,2},{9,3},... | collective-permute-start | bytes 540680 | tf_op jit(solution)/shard_map/ppermute | solution.py:257
  15.6 29.8 %collective-permute-start.5 = (f32[352,128]{1,0:T(8,128)S(1)}, f32[352,128]{1,0:T(8,128)S(1)}, u32[]{:S(2)}, u32[]{:S(2)}) collective-permute-start(f32[352,128]{1,0:T(8,128)S(1)} %bitcast.373), channel_id=1, source_target_pairs={{0,14},{1,15},{2,12},{3,13},{4,10},{5,11},{6,8},{7,9},{8,6},{9,7},... | collective-permute-start | bytes 540680 | tf_op jit(solution)/shard_map/ppermute | solution.py:257
  18.7 26.7 %collective-permute-start.6 = (f32[352,128]{1,0:T(8,128)S(1)}, f32[352,128]{1,0:T(8,128)S(1)}, u32[]{:S(2)}, u32[]{:S(2)}) collective-permute-start(f32[352,128]{1,0:T(8,128)S(1)} %bitcast.372), channel_id=1, source_target_pairs={{0,6},{1,7},{2,4},{3,5},{4,2},{5,3},{6,0},{7,1},{8,14},{9,15},{10,... | collective-permute-start | bytes 540680 | tf_op jit(solution)/shard_map/ppermute | solution.py:257
  24.6 20.8 %collective-permute-start.7 = (f32[352,128]{1,0:T(8,128)S(1)}, f32[352,128]{1,0:T(8,128)S(1)}, u32[]{:S(2)}, u32[]{:S(2)}) collective-permute-start(f32[352,128]{1,0:T(8,128)S(1)} %bitcast.371), channel_id=1, source_target_pairs={{0,2},{1,3},{2,0},{3,1},{4,6},{5,7},{6,4},{7,5},{8,10},{9,11},{10,... | collective-permute-start | bytes 540680 | tf_op jit(solution)/shard_map/ppermute | solution.py:257

commit v4 on v3

--- a/solution.py
+++ b/solution.py
@@ -15,6 +15,8 @@
 CHIRP_STEP = 3.0
 TINY = 1e-06
 PAD = 8
+CHUNK = 1024
+MOVED = 2
 F32 = jnp.float32
 BF16 = jnp.bfloat16
 
@@ -68,38 +70,16 @@
     coef[2] = 2.0 * ab / scale
 
 
-def one_stat(pair, side, drift, chirp, table, twist, prep, coef, moved):
-    rows = table.shape[0] // 2
+def shifted(both, amount, coef, moved):
+    rows = both[0].shape[1]
     halves = rows // BLK
-    sign = 1.0 if side == 0 else -1.0
-    cos, sin = chirp[0], chirp[1] * sign
-    left = jnp.concatenate([prep[2 * w] * cos + prep[2 * w + 1] * sin for w in (0, 1)], axis=1)
-    right = jnp.concatenate([prep[2 * w + 1] * cos - prep[2 * w] * sin for w in (0, 1)], axis=1)
-    weighted = jnp.concatenate([left.astype(BF16), right.astype(BF16)], axis=0)
-    one = jnp.dot(table[...], weighted, preferred_element_type=F32)
-    turn_cos, turn_sin = twist[0], twist[1]
-    spectra = []
-    for weight in range(2):
-        columns = slice(weight * rows, (weight + 1) * rows)
-        one_real, one_imag = one[:rows, columns], one[rows:, columns]
-        middle = jnp.concatenate(
-            [
-                (one_real * turn_cos + one_imag * turn_sin).astype(BF16),
-                (one_imag * turn_cos - one_real * turn_sin).astype(BF16),
-            ],
-            axis=1,
-        )
-        both = lax.dot_general(
-            table[...], middle, (((1,), (1,)), ((), ())), preferred_element_type=F32
-        )
-        spectra += [both[:rows], both[rows:]]
-    ar, ai, br, bi = spectra
+    ar, ai = both[0][:rows], both[0][rows:]
+    br, bi = both[1][:rows], both[1][rows:]
     energy = (
         coef[0] * (ar * ar + ai * ai)
         + coef[1] * (br * br + bi * bi)
         - coef[2] * (ar * br + ai * bi)
     )
-    amount = drift[0, level_of(pair, side)]
     moved[PAD : PAD + PAD] = jnp.zeros((PAD, BLK), F32)
     moved[PAD + halves * rows - PAD : PAD + halves * rows] = jnp.zeros((PAD, BLK), F32)
     for half in range(halves):
@@ -156,12 +136,49 @@
     for move in moves[2:]:
         move.wait()
     per = own.shape[2]
-    for index, (pair, side) in enumerate(kept):
-        at = chirp.at[pair - first_pair]
-        one_stat(pair, side, drift, at, table, twist, prep, coef, moved)
+    ones, spectra = {}, {}
+
+    def first_step(index, weight):
+        pair, side = kept[index]
+        cos, sin = chirp[pair - first_pair, 0], chirp[pair - first_pair, 1]
+        real, imag = prep[2 * weight], prep[2 * weight + 1]
+        rc, iS, ic, rs = real * cos, imag * sin, imag * cos, real * sin
+        left, right = (rc + iS, ic - rs) if side == 0 else (rc - iS, ic + rs)
+        both = jnp.concatenate([left.astype(BF16), right.astype(BF16)], axis=0)
+        ones[index, weight] = jnp.dot(table[...], both, preferred_element_type=F32)
+
+    def third_step(index, weight):
+        one = ones.pop((index, weight))
+        rows = one.shape[0] // 2
+        turn_cos, turn_sin = twist[0], twist[1]
+        one_real, one_imag = one[:rows], one[rows:]
+        middle = jnp.concatenate(
+            [
+                (one_real * turn_cos + one_imag * turn_sin).astype(BF16),
+                (one_imag * turn_cos - one_real * turn_sin).astype(BF16),
+            ],
+            axis=1,
+        )
+        spectra[index, weight] = lax.dot_general(
+            table[...], middle, (((1,), (1,)), ((), ())), preferred_element_type=F32
+        )
+
+    def fourth_step(index):
+        held = moved.at[index % MOVED]
+        both = [spectra.pop((index, weight)) for weight in range(2)]
+        shifted(both, drift[0, level_of(*kept[index])], coef, held)
         for away in range(count // 2):
-            own[index, away] = moved[block_of(count, per, away, 0), :]
-            give[index, away] = moved[block_of(count, per, away, 1), :]
+            own[index, away] = held[block_of(count, per, away, 0), :]
+            give[index, away] = held[block_of(count, per, away, 1), :]
+
+    for index in range(len(kept) + 1):
+        for weight in range(2):
+            if index < len(kept):
+                first_step(index, weight)
+            if index:
+                third_step(index - 1, weight)
+        if index:
+            fourth_step(index - 1)
 
 
 def stat(kept, limit, cost, count, drift, series, weights):
@@ -187,7 +204,7 @@
             pltpu.VMEM(series.shape, F32),
             pltpu.VMEM((4, rows, rows), F32),
             pltpu.SMEM((3,), F32),
-            pltpu.VMEM((points // BLK + 2 * PAD, BLK), F32),
+            pltpu.VMEM((MOVED, points // BLK + 2 * PAD, BLK), F32),
             pltpu.SMEM(drift.shape, jnp.int32),
             pltpu.SemaphoreType.DMA((6,)),
         ],
@@ -198,7 +215,7 @@
 
 def sum_kernel(plan, segments, has_start, tracks, meta, *refs):
     start = refs[0] if has_start else None
-    blocks, out, gathered = refs[has_start:-2], refs[-2], refs[-1]
+    blocks, (out, gathered, total, sems) = refs[has_start:-4], refs[-4:]
     total_rows = gathered.shape[0]
     width = gathered.shape[1]
     me = lax.axis_index("seg")
@@ -212,24 +229,35 @@
     )
     pick = jnp.where((named == level.astype(F32)) | (level < 0), 1.0, 0.0).astype(BF16)
     per = width // BLK
-    for column in range(per):
-        at = 0
-        for block, height in zip(blocks, plan):
-            gathered[at : at + height, column * BLK : (column + 1) * BLK] = block[
-                pl.ds(column, height, stride=per), :
-            ]
-            at += height
-    for column in range(0, width, 512):
-        size = min(512, width - column)
-        value = gathered[:, column : column + size]
+    size = min(CHUNK, width)
+    leave = []
+    for column in range(0, width, size):
+        here = slice(column, column + size)
+        for tile in range(column // BLK, (column + size) // BLK):
+            at = 0
+            for block, height in zip(blocks, plan):
+                gathered[at : at + height, tile * BLK : (tile + 1) * BLK] = block[
+                    pl.ds(tile, height, stride=per), :
+                ]
+                at += height
+        value = gathered[:, here]
         high = value.astype(BF16)
         low = (value - high.astype(F32)).astype(BF16)
-        total = jnp.dot(pick, high, preferred_element_type=F32)
-        total = total + jnp.dot(pick, low, preferred_element_type=F32)
-        total = total * (1.0 / segments)
+        result = jnp.dot(pick, high, preferred_element_type=F32)
+        result = result + jnp.dot(pick, low, preferred_element_type=F32)
+        result = result * (1.0 / segments)
         if has_start:
-            total = total + start[:, column : column + size]
-        out[:, column : column + size] = total
+            total[:, here] = result + start[:, here]
+            leave.append(
+                pltpu.make_async_copy(
+                    total.at[:, here], out.at[:, here], sems.at[column // size]
+                )
+            )
+            leave[-1].start()
+        else:
+            out[:, here] = result
+    for move in leave:
+        move.wait()
 
 
 def track_sum(tracks, parts, start=None):
@@ -238,10 +266,17 @@
     width = parts[0][0].shape[0] * BLK // plan[0]
     meta = np.array([row for _, levels in parts for row in levels]).T
     starts = [] if start is None else [start]
+    held = (ntrack, width) if starts else (8, BLK)
+    place = pltpu.HBM if starts else pltpu.VMEM
     return pl.pallas_call(
         functools.partial(sum_kernel, plan, segments, len(starts)),
         out_shape=jax.ShapeDtypeStruct((ntrack, width), F32),
-        scratch_shapes=[pltpu.VMEM((sum(plan), width), F32)],
+        out_specs=pl.BlockSpec(memory_space=place),
+        scratch_shapes=[
+            pltpu.VMEM((sum(plan), width), F32),
+            pltpu.VMEM(held, F32),
+            pltpu.SemaphoreType.DMA((max(1, width // CHUNK),)),
+        ],
         compiler_params=pltpu.CompilerParams(vmem_limit_bytes=32 * 2**20),
     )(tracks, jnp.asarray(meta, jnp.int32), *starts, *[block for block, _ in parts])
 

time: 47.6 us -> 46.4 us (0.975)
  Pallas kernels: 9.79 us -> 8.58 us
    pallas_call x1, Pallas kernels: 7.09 us -> 6.05 us  [stat(): pl.pallas_call(functools.partial(stat_kernel, kept, count), out_shape=(ja...]
where the time goes in v4:
time: 46.4 us; the launch traced here: 46 us
  waiting for transfers between devices  22 us (47%)
  starting transfers between devices  14.8 us (32%)
  Pallas kernels  8.58 us (18%)
    ppermute x8, waiting for transfers between devices, local(): lax.ppermute(array, 'seg', swap(hop))  22 us
    ppermute x8, starting transfers between devices, local(): lax.ppermute(array, 'seg', swap(hop))  14.8 us
    pallas_call x1, Pallas kernels, stat(): pl.pallas_call(functools.partial(stat_kernel, kept, count), out_shape=(ja...  6.05 us
    pallas_call x2, Pallas kernels, track_sum(): pl.pallas_call(functools.partial(sum_kernel, plan, segments, len(starts))...  2.53 us
  transfers between devices with their start and end apart: 8, of which 5 were waited for; matrix products, arithmetic and copies ran while one was open for 0% of the time, Pallas kernels for 2%

profile of v4, /device:TPU:16, one launch (start us, length us, event | category | flops | bytes accessed | tf_op | source)
XLA Modules:
  0.0 46.0 jit_solution(14970498066503162933)
XLA Ops:
  0.0 6.0 %shard_map.91 = (f32[6,8,32,128]{3,2,1,0:T(8,128)S(1)}, f32[6,8,32,128]{3,2,1,0:T(8,128)S(1)}) custom-call(s32[1,6]{1,0:T(1,128)} %drift_hbm.1, bf16[1024,128]{1,0:T(8,128)(2,1)} %bitcast.379, f32[1024,128]{1,0:T(8,128)} %bitcast.378, bf16[512,512]{1,0:T(8,128)(2,1)} %constant.18.table_hbm, f32[2,256,256]{2,1,0:T(8,128)} %constant.11.clone.twist_hbm, ...), custom_call_target="tpu_custom_call" | custom-call | flops 1000000000 | bytes 3145728 | tf_op jit(solution)/shard_map/pallas_call | solution.py:193
  6.1 0.1 collective-permute-start
  6.2 2.2 %collective-permute-done = f32[6,8,32,128]{3,2,1,0:T(8,128)S(1)} collective-permute-done((f32[6,8,32,128]{3,2,1,0:T(8,128)S(1)}, f32[6,8,32,128]{3,2,1,0:T(8,128)S(1)}, u32[]{:S(2)}, u32[]{:S(2)}) %collective-permute-start) | collective-permute-done | bytes 786464 | tf_op jit(solution)/shard_map/ppermute | solution.py:292
  8.4 0.1 slice_subtract_fusion
  8.6 0.0 copy-start.2
  8.6 0.0 copy-start.1
  8.7 0.0 copy-start
  8.8 0.1 collective-permute-start.1
  8.9 1.9 %collective-permute-start.2 = (f32[352,128]{1,0:T(8,128)S(1)}, f32[352,128]{1,0:T(8,128)S(1)}, u32[]{:S(2)}, u32[]{:S(2)}) collective-permute-start(f32[352,128]{1,0:T(8,128)S(1)} %bitcast.376), channel_id=1, source_target_pairs={{0,4},{1,5},{2,6},{3,7},{4,0},{5,1},{6,2},{7,3},{8,12},{9,13},{10,... | collective-permute-start | bytes 540680 | tf_op jit(solution)/shard_map/ppermute | solution.py:292
  10.8 1.6 %collective-permute-start.3 = (f32[352,128]{1,0:T(8,128)S(1)}, f32[352,128]{1,0:T(8,128)S(1)}, u32[]{:S(2)}, u32[]{:S(2)}) collective-permute-start(f32[352,128]{1,0:T(8,128)S(1)} %bitcast.375), channel_id=1, source_target_pairs={{0,12},{1,13},{2,14},{3,15},{4,8},{5,9},{6,10},{7,11},{8,4},{9,5},... | collective-permute-start | bytes 540680 | tf_op jit(solution)/shard_map/ppermute | solution.py:292
  12.4 2.2 %collective-permute-start.4 = (f32[352,128]{1,0:T(8,128)S(1)}, f32[352,128]{1,0:T(8,128)S(1)}, u32[]{:S(2)}, u32[]{:S(2)}) collective-permute-start(f32[352,128]{1,0:T(8,128)S(1)} %bitcast.374), channel_id=1, source_target_pairs={{0,10},{1,11},{2,8},{3,9},{4,14},{5,15},{6,12},{7,13},{8,2},{9,3},... | collective-permute-start | bytes 540680 | tf_op jit(solution)/shard_map/ppermute | solution.py:292
  14.6 2.7 %collective-permute-start.5 = (f32[352,128]{1,0:T(8,128)S(1)}, f32[352,128]{1,0:T(8,128)S(1)}, u32[]{:S(2)}, u32[]{:S(2)}) collective-permute-start(f32[352,128]{1,0:T(8,128)S(1)} %bitcast.373), channel_id=1, source_target_pairs={{0,14},{1,15},{2,12},{3,13},{4,10},{5,11},{6,8},{7,9},{8,6},{9,7},... | collective-permute-start | bytes 540680 | tf_op jit(solution)/shard_map/ppermute | solution.py:292
  17.2 0.5 collective-permute-done.1.refs_1_
  17.7 5.9 %collective-permute-start.6 = (f32[352,128]{1,0:T(8,128)S(1)}, f32[352,128]{1,0:T(8,128)S(1)}, u32[]{:S(2)}, u32[]{:S(2)}) collective-permute-start(f32[352,128]{1,0:T(8,128)S(1)} %bitcast.372), channel_id=1, source_target_pairs={{0,6},{1,7},{2,4},{3,5},{4,2},{5,3},{6,0},{7,1},{8,14},{9,15},{10,... | collective-permute-start | bytes 540680 | tf_op jit(solution)/shard_map/ppermute | solution.py:292
  23.6 0.0 collective-permute-done.2.refs_2_
  23.6 0.5 %collective-permute-start.7 = (f32[352,128]{1,0:T(8,128)S(1)}, f32[352,128]{1,0:T(8,128)S(1)}, u32[]{:S(2)}, u32[]{:S(2)}) collective-permute-start(f32[352,128]{1,0:T(8,128)S(1)} %bitcast.371), channel_id=1, source_target_pairs={{0,2},{1,3},{2,0},{3,1},{4,6},{5,7},{6,4},{7,5},{8,10},{9,11},{10,... | collective-permute-start | bytes 540680 | tf_op jit(solution)/shard_map/ppermute | solution.py:292
  24.1 0.0 copy-done.2
  24.1 0.1 copy.13.tracks
  24.2 11.6 %collective-permute-done.3.refs_3_ = f32[352,128]{1,0:T(8,128)S(1)} collective-permute-done((f32[352,128]{1,0:T(8,128)S(1)}, f32[352,128]{1,0:T(8,128)S(1)}, u32[]{:S(2)}, u32[]{:S(2)}) %collective-permute-start.3) | collective-permute-done | bytes 180256 | tf_op jit(solution)/shard_map/ppermute | solution.py:292
  35.8 0.0 copy-done.1
  35.8 0.9 %shard_map.92.refs_0_ = f32[64,4096]{1,0:T(8,128)S(1)} custom-call(s32[64,16]{1,0:T(8,128)S(1)} %copy.13.tracks, s32[3,44]{1,0:T(4,128)S(1)} %copy-done.1, f32[352,128]{1,0:T(8,128)S(1)} %bitcast.370, f32[352,128]{1,0:T(8,128)S(1)} %collective-permute-done.1.refs_1_, f32[352,128]{1,0:T(8,128)S(1)} %collective-permute-done.2.refs_2_, ...), custom_call_target="tpu_custom_call" | custom-call | tf_op jit(solution)/shard_map/pallas_call | solution.py:271
  36.7 0.3 collective-permute-done.4.refs_1_
  37.0 7.4 %collective-permute-done.5.refs_2_ = f32[352,128]{1,0:T(8,128)S(1)} collective-permute-done((f32[352,128]{1,0:T(8,128)S(1)}, f32[352,128]{1,0:T(8,128)S(1)}, u32[]{:S(2)}, u32[]{:S(2)}) %collective-permute-start.5) | collective-permute-done | bytes 180256 | tf_op jit(solution)/shard_map/ppermute | solution.py:292
  44.4 0.0 collective-permute-done.6.refs_3_
  44.4 0.0 collective-permute-done.7.refs_4_
  44.4 0.0 copy-done
  44.4 1.6 %shard_map.93 = f32[64,4096]{1,0:T(8,128)} custom-call(s32[64,16]{1,0:T(8,128)S(1)} %copy.13.tracks, s32[3,44]{1,0:T(4,128)S(1)} %copy-done, f32[64,4096]{1,0:T(8,128)S(1)} %shard_map.92.refs_0_, f32[352,128]{1,0:T(8,128)S(1)} %collective-permute-done.4.refs_1_, f32[352,128]{1,0:T(8,128)S(1)} %collective-permute-done.5.refs_2_, ...), custom_call_target="tpu_custom_call" | custom-call | tf_op jit(solution)/shard_map/pallas_call | solution.py:271
  (12 shorter events, 0.2 us)
Async XLA Ops:
  6.1 2.4 %collective-permute-start = (f32[6,8,32,128]{3,2,1,0:T(8,128)S(1)}, f32[6,8,32,128]{3,2,1,0:T(8,128)S(1)}, u32[]{:S(2)}, u32[]{:S(2)}) collective-permute-start(f32[6,8,32,128]{3,2,1,0:T(8,128)S(1)} %get-tuple-element.8), channel_id=1, source_target_pairs={{0,1},{1,0},{2,3},{3,2},{4,5},{5,4},{6,7},{7,6},{8,9},{9,8},{10,11... | collective-permute-start | bytes 2359304 | tf_op jit(solution)/shard_map/ppermute | solution.py:292
  8.6 15.5 %copy-start.2 = (s32[64,16]{0,1:T(8,128)S(1)}, s32[64,16]{0,1:T(8,128)}, u32[]{:S(2)}) copy-start(s32[64,16]{0,1:T(8,128)} %param.12) | copy-start | bytes 12292
  8.6 27.2 %copy-start.1 = (s32[3,44]{1,0:T(4,128)S(1)}, s32[3,44]{1,0:T(4,128)}, u32[]{:S(2)}) copy-start(s32[3,44]{1,0:T(4,128)} %constant.13.clone.meta) | copy-start | bytes 1588
  8.7 35.7 %copy-start = (s32[3,44]{1,0:T(4,128)S(1)}, s32[3,44]{1,0:T(4,128)}, u32[]{:S(2)}) copy-start(s32[3,44]{1,0:T(4,128)} %constant.14.clone.meta) | copy-start | bytes 1588
  8.8 8.9 %collective-permute-start.1 = (f32[352,128]{1,0:T(8,128)S(1)}, f32[352,128]{1,0:T(8,128)S(1)}, u32[]{:S(2)}, u32[]{:S(2)}) collective-permute-start(f32[352,128]{1,0:T(8,128)S(1)} %bitcast.377), channel_id=1, source_target_pairs={{0,8},{1,9},{2,10},{3,11},{4,12},{5,13},{6,14},{7,15},{8,0},{9,1},... | collective-permute-start | bytes 540680 | tf_op jit(solution)/shard_map/ppermute | solution.py:292
  8.9 14.7 %collective-permute-start.2 = (f32[352,128]{1,0:T(8,128)S(1)}, f32[352,128]{1,0:T(8,128)S(1)}, u32[]{:S(2)}, u32[]{:S(2)}) collective-permute-start(f32[352,128]{1,0:T(8,128)S(1)} %bitcast.376), channel_id=1, source_target_pairs={{0,4},{1,5},{2,6},{3,7},{4,0},{5,1},{6,2},{7,3},{8,12},{9,13},{10,... | collective-permute-start | bytes 540680 | tf_op jit(solution)/shard_map/ppermute | solution.py:292
  10.8 25.0 %collective-permute-start.3 = (f32[352,128]{1,0:T(8,128)S(1)}, f32[352,128]{1,0:T(8,128)S(1)}, u32[]{:S(2)}, u32[]{:S(2)}) collective-permute-start(f32[352,128]{1,0:T(8,128)S(1)} %bitcast.375), channel_id=1, source_target_pairs={{0,12},{1,13},{2,14},{3,15},{4,8},{5,9},{6,10},{7,11},{8,4},{9,5},... | collective-permute-start | bytes 540680 | tf_op jit(solution)/shard_map/ppermute | solution.py:292
  12.4 24.6 %collective-permute-start.4 = (f32[352,128]{1,0:T(8,128)S(1)}, f32[352,128]{1,0:T(8,128)S(1)}, u32[]{:S(2)}, u32[]{:S(2)}) collective-permute-start(f32[352,128]{1,0:T(8,128)S(1)} %bitcast.374), channel_id=1, source_target_pairs={{0,10},{1,11},{2,8},{3,9},{4,14},{5,15},{6,12},{7,13},{8,2},{9,3},... | collective-permute-start | bytes 540680 | tf_op jit(solution)/shard_map/ppermute | solution.py:292
  14.6 29.8 %collective-permute-start.5 = (f32[352,128]{1,0:T(8,128)S(1)}, f32[352,128]{1,0:T(8,128)S(1)}, u32[]{:S(2)}, u32[]{:S(2)}) collective-permute-start(f32[352,128]{1,0:T(8,128)S(1)} %bitcast.373), channel_id=1, source_target_pairs={{0,14},{1,15},{2,12},{3,13},{4,10},{5,11},{6,8},{7,9},{8,6},{9,7},... | collective-permute-start | bytes 540680 | tf_op jit(solution)/shard_map/ppermute | solution.py:292
  17.7 26.7 %collective-permute-start.6 = (f32[352,128]{1,0:T(8,128)S(1)}, f32[352,128]{1,0:T(8,128)S(1)}, u32[]{:S(2)}, u32[]{:S(2)}) collective-permute-start(f32[352,128]{1,0:T(8,128)S(1)} %bitcast.372), channel_id=1, source_target_pairs={{0,6},{1,7},{2,4},{3,5},{4,2},{5,3},{6,0},{7,1},{8,14},{9,15},{10,... | collective-permute-start | bytes 540680 | tf_op jit(solution)/shard_map/ppermute | solution.py:292
  23.6 20.8 %collective-permute-start.7 = (f32[352,128]{1,0:T(8,128)S(1)}, f32[352,128]{1,0:T(8,128)S(1)}, u32[]{:S(2)}, u32[]{:S(2)}) collective-permute-start(f32[352,128]{1,0:T(8,128)S(1)} %bitcast.371), channel_id=1, source_target_pairs={{0,2},{1,3},{2,0},{3,1},{4,6},{5,7},{6,4},{7,5},{8,10},{9,11},{10,... | collective-permute-start | bytes 540680 | tf_op jit(solution)/shard_map/ppermute | solution.py:292

commit v5 on v4

--- a/solution.py
+++ b/solution.py
@@ -287,7 +287,10 @@
     series, weights = tile(strain_series), tile(antenna)
     chips = count // 2
     half = chips // 2
-    far, near = range(half, chips), range(half)
+    even_first = lambda away: (away % 2, away)
+    far, near = sorted(range(half, chips), key=even_first), sorted(range(1, half), key=even_first)
+    order = [0] + far[:1] + near[:1] + far[1:] + near[:0:-1]
+    early = order[: 1 + half - half // 4]
     swap = lambda hop: [(device, device ^ hop) for device in range(count)]
     send = lambda array, hop: lax.ppermute(array, "seg", swap(hop)) if hop else array
     pack = lambda rows: jnp.stack(rows).reshape(-1, BLK)
@@ -299,13 +302,13 @@
         for other, part in enumerate((own, got)):
             rows.append(part[1 + index] - part[0])
             names.append((level_of(pair, side), other))
-    blocks = {away: send(pack([row[away] for row in rows]), 2 * away) for away in (0,4,2,6,5,7,3,1)}
+    blocks = {away: send(pack([row[away] for row in rows]), 2 * away) for away in order}
     parts = {
         away: (block, [(level, other, away) for level, other in names])
         for away, block in blocks.items()
     }
-    first = [parts[away] for away in (0,4,2,6)]
-    last = [parts[away] for away in (0,4,2,6,5,7,3,1) if away not in (0,4,2,6)]
+    first = [parts[away] for away in early]
+    last = [parts[away] for away in order if away not in early]
     return track_sum(tracks, last, track_sum(tracks, first))
 
 

time: 46.4 us -> 46.4 us (level)
  no operation moved by 1% of the time
where the time goes in v5:
time: 46.4 us; the launch traced here: 46 us
  waiting for transfers between devices  22 us (47%)
  starting transfers between devices  14.8 us (32%)
  Pallas kernels  8.58 us (18%)
    ppermute x8, waiting for transfers between devices, local(): lax.ppermute(array, 'seg', swap(hop))  22 us
    ppermute x8, starting transfers between devices, local(): lax.ppermute(array, 'seg', swap(hop))  14.8 us
    pallas_call x1, Pallas kernels, stat(): pl.pallas_call(functools.partial(stat_kernel, kept, count), out_shape=(ja...  6.05 us
    pallas_call x2, Pallas kernels, track_sum(): pl.pallas_call(functools.partial(sum_kernel, plan, segments, len(starts))...  2.53 us
  transfers between devices with their start and end apart: 8, of which 5 were waited for; matrix products, arithmetic and copies ran while one was open for 0% of the time, Pallas kernels for 2%

profile of v5, /device:TPU:16, one launch (start us, length us, event | category | flops | bytes accessed | tf_op | source)
XLA Modules:
  0.0 46.0 jit_solution(14970498066503162933)
XLA Ops:
  0.0 6.0 %shard_map.91 = (f32[6,8,32,128]{3,2,1,0:T(8,128)S(1)}, f32[6,8,32,128]{3,2,1,0:T(8,128)S(1)}) custom-call(s32[1,6]{1,0:T(1,128)} %drift_hbm.1, bf16[1024,128]{1,0:T(8,128)(2,1)} %bitcast.379, f32[1024,128]{1,0:T(8,128)} %bitcast.378, bf16[512,512]{1,0:T(8,128)(2,1)} %constant.18.table_hbm, f32[2,256,256]{2,1,0:T(8,128)} %constant.11.clone.twist_hbm, ...), custom_call_target="tpu_custom_call" | custom-call | flops 1000000000 | bytes 3145728 | tf_op jit(solution)/shard_map/pallas_call | solution.py:193
  6.1 0.1 collective-permute-start
  6.2 2.2 %collective-permute-done = f32[6,8,32,128]{3,2,1,0:T(8,128)S(1)} collective-permute-done((f32[6,8,32,128]{3,2,1,0:T(8,128)S(1)}, f32[6,8,32,128]{3,2,1,0:T(8,128)S(1)}, u32[]{:S(2)}, u32[]{:S(2)}) %collective-permute-start) | collective-permute-done | bytes 786464 | tf_op jit(solution)/shard_map/ppermute | solution.py:295
  8.4 0.1 slice_subtract_fusion
  8.6 0.0 copy-start.2
  8.6 0.0 copy-start.1
  8.7 0.0 copy-start
  8.8 0.1 collective-permute-start.1
  8.9 1.9 %collective-permute-start.2 = (f32[352,128]{1,0:T(8,128)S(1)}, f32[352,128]{1,0:T(8,128)S(1)}, u32[]{:S(2)}, u32[]{:S(2)}) collective-permute-start(f32[352,128]{1,0:T(8,128)S(1)} %bitcast.376), channel_id=1, source_target_pairs={{0,4},{1,5},{2,6},{3,7},{4,0},{5,1},{6,2},{7,3},{8,12},{9,13},{10,... | collective-permute-start | bytes 540680 | tf_op jit(solution)/shard_map/ppermute | solution.py:295
  10.8 1.6 %collective-permute-start.3 = (f32[352,128]{1,0:T(8,128)S(1)}, f32[352,128]{1,0:T(8,128)S(1)}, u32[]{:S(2)}, u32[]{:S(2)}) collective-permute-start(f32[352,128]{1,0:T(8,128)S(1)} %bitcast.375), channel_id=1, source_target_pairs={{0,12},{1,13},{2,14},{3,15},{4,8},{5,9},{6,10},{7,11},{8,4},{9,5},... | collective-permute-start | bytes 540680 | tf_op jit(solution)/shard_map/ppermute | solution.py:295
  12.4 2.2 %collective-permute-start.4 = (f32[352,128]{1,0:T(8,128)S(1)}, f32[352,128]{1,0:T(8,128)S(1)}, u32[]{:S(2)}, u32[]{:S(2)}) collective-permute-start(f32[352,128]{1,0:T(8,128)S(1)} %bitcast.374), channel_id=1, source_target_pairs={{0,10},{1,11},{2,8},{3,9},{4,14},{5,15},{6,12},{7,13},{8,2},{9,3},... | collective-permute-start | bytes 540680 | tf_op jit(solution)/shard_map/ppermute | solution.py:295
  14.6 2.7 %collective-permute-start.5 = (f32[352,128]{1,0:T(8,128)S(1)}, f32[352,128]{1,0:T(8,128)S(1)}, u32[]{:S(2)}, u32[]{:S(2)}) collective-permute-start(f32[352,128]{1,0:T(8,128)S(1)} %bitcast.373), channel_id=1, source_target_pairs={{0,14},{1,15},{2,12},{3,13},{4,10},{5,11},{6,8},{7,9},{8,6},{9,7},... | collective-permute-start | bytes 540680 | tf_op jit(solution)/shard_map/ppermute | solution.py:295
  17.2 0.5 collective-permute-done.1.refs_1_
  17.7 5.9 %collective-permute-start.6 = (f32[352,128]{1,0:T(8,128)S(1)}, f32[352,128]{1,0:T(8,128)S(1)}, u32[]{:S(2)}, u32[]{:S(2)}) collective-permute-start(f32[352,128]{1,0:T(8,128)S(1)} %bitcast.372), channel_id=1, source_target_pairs={{0,6},{1,7},{2,4},{3,5},{4,2},{5,3},{6,0},{7,1},{8,14},{9,15},{10,... | collective-permute-start | bytes 540680 | tf_op jit(solution)/shard_map/ppermute | solution.py:295
  23.6 0.0 collective-permute-done.2.refs_2_
  23.6 0.5 %collective-permute-start.7 = (f32[352,128]{1,0:T(8,128)S(1)}, f32[352,128]{1,0:T(8,128)S(1)}, u32[]{:S(2)}, u32[]{:S(2)}) collective-permute-start(f32[352,128]{1,0:T(8,128)S(1)} %bitcast.371), channel_id=1, source_target_pairs={{0,2},{1,3},{2,0},{3,1},{4,6},{5,7},{6,4},{7,5},{8,10},{9,11},{10,... | collective-permute-start | bytes 540680 | tf_op jit(solution)/shard_map/ppermute | solution.py:295
  24.1 0.0 copy-done.2
  24.1 0.1 copy.13.tracks
  24.2 11.6 %collective-permute-done.3.refs_3_ = f32[352,128]{1,0:T(8,128)S(1)} collective-permute-done((f32[352,128]{1,0:T(8,128)S(1)}, f32[352,128]{1,0:T(8,128)S(1)}, u32[]{:S(2)}, u32[]{:S(2)}) %collective-permute-start.3) | collective-permute-done | bytes 180256 | tf_op jit(solution)/shard_map/ppermute | solution.py:295
  35.8 0.0 copy-done.1
  35.8 0.9 %shard_map.92.refs_0_ = f32[64,4096]{1,0:T(8,128)S(1)} custom-call(s32[64,16]{1,0:T(8,128)S(1)} %copy.13.tracks, s32[3,44]{1,0:T(4,128)S(1)} %copy-done.1, f32[352,128]{1,0:T(8,128)S(1)} %bitcast.370, f32[352,128]{1,0:T(8,128)S(1)} %collective-permute-done.1.refs_1_, f32[352,128]{1,0:T(8,128)S(1)} %collective-permute-done.2.refs_2_, ...), custom_call_target="tpu_custom_call" | custom-call | tf_op jit(solution)/shard_map/pallas_call | solution.py:271
  36.7 0.3 collective-permute-done.4.refs_1_
  37.0 7.4 %collective-permute-done.5.refs_2_ = f32[352,128]{1,0:T(8,128)S(1)} collective-permute-done((f32[352,128]{1,0:T(8,128)S(1)}, f32[352,128]{1,0:T(8,128)S(1)}, u32[]{:S(2)}, u32[]{:S(2)}) %collective-permute-start.5) | collective-permute-done | bytes 180256 | tf_op jit(solution)/shard_map/ppermute | solution.py:295
  44.4 0.0 collective-permute-done.6.refs_3_
  44.4 0.0 collective-permute-done.7.refs_4_
  44.4 0.0 copy-done
  44.4 1.6 %shard_map.93 = f32[64,4096]{1,0:T(8,128)} custom-call(s32[64,16]{1,0:T(8,128)S(1)} %copy.13.tracks, s32[3,44]{1,0:T(4,128)S(1)} %copy-done, f32[64,4096]{1,0:T(8,128)S(1)} %shard_map.92.refs_0_, f32[352,128]{1,0:T(8,128)S(1)} %collective-permute-done.4.refs_1_, f32[352,128]{1,0:T(8,128)S(1)} %collective-permute-done.5.refs_2_, ...), custom_call_target="tpu_custom_call" | custom-call | tf_op jit(solution)/shard_map/pallas_call | solution.py:271
  (12 shorter events, 0.2 us)
Async XLA Ops:
  6.1 2.4 %collective-permute-start = (f32[6,8,32,128]{3,2,1,0:T(8,128)S(1)}, f32[6,8,32,128]{3,2,1,0:T(8,128)S(1)}, u32[]{:S(2)}, u32[]{:S(2)}) collective-permute-start(f32[6,8,32,128]{3,2,1,0:T(8,128)S(1)} %get-tuple-element.8), channel_id=1, source_target_pairs={{0,1},{1,0},{2,3},{3,2},{4,5},{5,4},{6,7},{7,6},{8,9},{9,8},{10,11... | collective-permute-start | bytes 2359304 | tf_op jit(solution)/shard_map/ppermute | solution.py:295
  8.6 15.5 %copy-start.2 = (s32[64,16]{0,1:T(8,128)S(1)}, s32[64,16]{0,1:T(8,128)}, u32[]{:S(2)}) copy-start(s32[64,16]{0,1:T(8,128)} %param.12) | copy-start | bytes 12292
  8.6 27.2 %copy-start.1 = (s32[3,44]{1,0:T(4,128)S(1)}, s32[3,44]{1,0:T(4,128)}, u32[]{:S(2)}) copy-start(s32[3,44]{1,0:T(4,128)} %constant.13.clone.meta) | copy-start | bytes 1588
  8.7 35.7 %copy-start = (s32[3,44]{1,0:T(4,128)S(1)}, s32[3,44]{1,0:T(4,128)}, u32[]{:S(2)}) copy-start(s32[3,44]{1,0:T(4,128)} %constant.14.clone.meta) | copy-start | bytes 1588
  8.8 8.9 %collective-permute-start.1 = (f32[352,128]{1,0:T(8,128)S(1)}, f32[352,128]{1,0:T(8,128)S(1)}, u32[]{:S(2)}, u32[]{:S(2)}) collective-permute-start(f32[352,128]{1,0:T(8,128)S(1)} %bitcast.377), channel_id=1, source_target_pairs={{0,8},{1,9},{2,10},{3,11},{4,12},{5,13},{6,14},{7,15},{8,0},{9,1},... | collective-permute-start | bytes 540680 | tf_op jit(solution)/shard_map/ppermute | solution.py:295
  8.9 14.7 %collective-permute-start.2 = (f32[352,128]{1,0:T(8,128)S(1)}, f32[352,128]{1,0:T(8,128)S(1)}, u32[]{:S(2)}, u32[]{:S(2)}) collective-permute-start(f32[352,128]{1,0:T(8,128)S(1)} %bitcast.376), channel_id=1, source_target_pairs={{0,4},{1,5},{2,6},{3,7},{4,0},{5,1},{6,2},{7,3},{8,12},{9,13},{10,... | collective-permute-start | bytes 540680 | tf_op jit(solution)/shard_map/ppermute | solution.py:295
  10.8 25.0 %collective-permute-start.3 = (f32[352,128]{1,0:T(8,128)S(1)}, f32[352,128]{1,0:T(8,128)S(1)}, u32[]{:S(2)}, u32[]{:S(2)}) collective-permute-start(f32[352,128]{1,0:T(8,128)S(1)} %bitcast.375), channel_id=1, source_target_pairs={{0,12},{1,13},{2,14},{3,15},{4,8},{5,9},{6,10},{7,11},{8,4},{9,5},... | collective-permute-start | bytes 540680 | tf_op jit(solution)/shard_map/ppermute | solution.py:295
  12.4 24.6 %collective-permute-start.4 = (f32[352,128]{1,0:T(8,128)S(1)}, f32[352,128]{1,0:T(8,128)S(1)}, u32[]{:S(2)}, u32[]{:S(2)}) collective-permute-start(f32[352,128]{1,0:T(8,128)S(1)} %bitcast.374), channel_id=1, source_target_pairs={{0,10},{1,11},{2,8},{3,9},{4,14},{5,15},{6,12},{7,13},{8,2},{9,3},... | collective-permute-start | bytes 540680 | tf_op jit(solution)/shard_map/ppermute | solution.py:295
  14.6 29.8 %collective-permute-start.5 = (f32[352,128]{1,0:T(8,128)S(1)}, f32[352,128]{1,0:T(8,128)S(1)}, u32[]{:S(2)}, u32[]{:S(2)}) collective-permute-start(f32[352,128]{1,0:T(8,128)S(1)} %bitcast.373), channel_id=1, source_target_pairs={{0,14},{1,15},{2,12},{3,13},{4,10},{5,11},{6,8},{7,9},{8,6},{9,7},... | collective-permute-start | bytes 540680 | tf_op jit(solution)/shard_map/ppermute | solution.py:295
  17.7 26.7 %collective-permute-start.6 = (f32[352,128]{1,0:T(8,128)S(1)}, f32[352,128]{1,0:T(8,128)S(1)}, u32[]{:S(2)}, u32[]{:S(2)}) collective-permute-start(f32[352,128]{1,0:T(8,128)S(1)} %bitcast.372), channel_id=1, source_target_pairs={{0,6},{1,7},{2,4},{3,5},{4,2},{5,3},{6,0},{7,1},{8,14},{9,15},{10,... | collective-permute-start | bytes 540680 | tf_op jit(solution)/shard_map/ppermute | solution.py:295
  23.6 20.8 %collective-permute-start.7 = (f32[352,128]{1,0:T(8,128)S(1)}, f32[352,128]{1,0:T(8,128)S(1)}, u32[]{:S(2)}, u32[]{:S(2)}) collective-permute-start(f32[352,128]{1,0:T(8,128)S(1)} %bitcast.371), channel_id=1, source_target_pairs={{0,2},{1,3},{2,0},{3,1},{4,6},{5,7},{6,4},{7,5},{8,10},{9,11},{10,... | collective-permute-start | bytes 540680 | tf_op jit(solution)/shard_map/ppermute | solution.py:295

commit v6 on v5

--- a/solution.py
+++ b/solution.py
@@ -113,8 +113,8 @@
 
 
 def stat_kernel(
-    kept, count, drift_hbm, series_hbm, weights_hbm, table_hbm, twist_hbm, chirp_hbm,
-    own, give,
+    kept, direct, count, drift_hbm, series_hbm, weights_hbm, table_hbm, twist_hbm, chirp_hbm,
+    own, give, both_cores,
     series, weights, table, twist, chirp, lanes, prep, coef, moved, drift, sems,
 ):
     first_pair = min(pair for pair, _ in kept)
@@ -167,9 +167,12 @@
         held = moved.at[index % MOVED]
         both = [spectra.pop((index, weight)) for weight in range(2)]
         shifted(both, drift[0, level_of(*kept[index])], coef, held)
-        for away in range(count // 2):
-            own[index, away] = held[block_of(count, per, away, 0), :]
-            give[index, away] = held[block_of(count, per, away, 1), :]
+        for other in range(2):
+            value = held[block_of(count, per, direct, other), :]
+            both_cores[other, index] = value - both_cores[other, 0] if index else value
+        for at, away in enumerate(others_of(count, direct)):
+            own[index, at] = held[block_of(count, per, away, 0), :]
+            give[index, at] = held[block_of(count, per, away, 1), :]
 
     for index in range(len(kept) + 1):
         for weight in range(2):
@@ -181,7 +184,11 @@
             fourth_step(index - 1)
 
 
-def stat(kept, limit, cost, count, drift, series, weights):
+def others_of(count, direct):
+    return [away for away in range(count // 2) if away != direct]
+
+
+def stat(kept, direct, limit, cost, count, drift, series, weights):
     points = series.shape[0] * BLK // 2
     rows = math.isqrt(points)
     per = points // BLK // count
@@ -189,12 +196,12 @@
     pairs = tuple(sorted({pair for pair, _ in kept}))
     inputs = (drift, series, weights, dft_table(rows), twist_table(rows), chirp_table(rows, pairs))
     hbm = pl.BlockSpec(memory_space=pltpu.HBM)
-    shape = (len(kept), chips, per, BLK)
+    shapes = [(len(kept), chips - 1, per, BLK)] * 2 + [(2, len(kept), per, BLK)]
     return pl.pallas_call(
-        functools.partial(stat_kernel, kept, count),
-        out_shape=(jax.ShapeDtypeStruct(shape, F32),) * 2,
+        functools.partial(stat_kernel, kept, direct, count),
+        out_shape=tuple(jax.ShapeDtypeStruct(shape, F32) for shape in shapes),
         in_specs=[hbm] * 6,
-        out_specs=(pl.BlockSpec(memory_space=pltpu.VMEM),) * 2,
+        out_specs=(pl.BlockSpec(memory_space=pltpu.VMEM),) * 3,
         scratch_shapes=[
             pltpu.VMEM(series.shape, BF16),
             pltpu.VMEM(weights.shape, F32),
@@ -288,27 +295,37 @@
     chips = count // 2
     half = chips // 2
     even_first = lambda away: (away % 2, away)
-    far, near = sorted(range(half, chips), key=even_first), sorted(range(1, half), key=even_first)
+    far, near = sorted(range(half, chips), key=even_first), list(range(1, half))
     order = [0] + far[:1] + near[:1] + far[1:] + near[:0:-1]
     early = order[: 1 + half - half // 4]
     swap = lambda hop: [(device, device ^ hop) for device in range(count)]
     send = lambda array, hop: lax.ppermute(array, "seg", swap(hop)) if hop else array
     pack = lambda rows: jnp.stack(rows).reshape(-1, BLK)
 
-    own, give = stat(EARLY, 32, 10**9, count, drift, series, weights)
+    direct = order[1]
+    own, give, both_cores = stat(EARLY, direct, 32, 10**9, count, drift, series, weights)
+    straight = send(both_cores, 2 * direct)
     got = send(give, 1)
     rows, names = [own[0] + got[0]], [(-1, 0)]
     for index, (pair, side) in enumerate(EARLY[1:]):
         for other, part in enumerate((own, got)):
             rows.append(part[1 + index] - part[0])
             names.append((level_of(pair, side), other))
-    blocks = {away: send(pack([row[away] for row in rows]), 2 * away) for away in order}
-    parts = {
-        away: (block, [(level, other, away) for level, other in names])
-        for away, block in blocks.items()
-    }
-    first = [parts[away] for away in early]
-    last = [parts[away] for away in order if away not in early]
+    place = {away: at for at, away in enumerate(others_of(count, direct))}
+    parts = {}
+    for away in order:
+        if away == direct:
+            continue
+        block = send(pack([row[place[away]] for row in rows]), 2 * away)
+        parts[away] = [(block, [(level, other, away) for level, other in names])]
+    straight, _ = lax.optimization_barrier((straight, parts[near[-1]][0][0] if near else straight))
+    levels = [-1] + [level_of(pair, side) for pair, side in EARLY[1:]]
+    parts[direct] = [
+        (block.reshape(-1, BLK), [(level, other, direct) for level in levels])
+        for other, block in enumerate((straight[0], send(straight[1], 1)))
+    ]
+    first = [part for away in early for part in parts[away]]
+    last = [part for away in order if away not in early for part in parts[away]]
     return track_sum(tracks, last, track_sum(tracks, first))
 
 

time: 46.4 us -> 44.9 us (0.968)
  waiting for transfers between devices: 22 us -> 16 us
  starting transfers between devices: 14.8 us -> 19.2 us
    ppermute x8 -> x9, waiting for transfers between devices: 22 us -> 16 us  [local(): lax.ppermute(array, 'seg', swap(hop))]
    ppermute x8 -> x9, starting transfers between devices: 14.8 us -> 19.2 us  [local(): lax.ppermute(array, 'seg', swap(hop))]
  transfers between devices with their start and end apart: 8 -> 9, of which waited for: 5 -> 5; matrix products, arithmetic and copies ran while one was open for 0% -> 1% of each run, Pallas kernels for 2% -> 2%
where the time goes in v6:
time: 44.9 us; the launch traced here: 44.4 us
  starting transfers between devices  19.2 us (43%)
  waiting for transfers between devices  16 us (36%)
  Pallas kernels  8.64 us (19%)
    ppermute x9, starting transfers between devices, local(): lax.ppermute(array, 'seg', swap(hop))  19.2 us
    ppermute x9, waiting for transfers between devices, local(): lax.ppermute(array, 'seg', swap(hop))  16 us
    pallas_call x1, Pallas kernels, stat(): pl.pallas_call(functools.partial(stat_kernel, kept, direct, count), out_s...  6.06 us
    pallas_call x2, Pallas kernels, track_sum(): pl.pallas_call(functools.partial(sum_kernel, plan, segments, len(starts))...  2.58 us
  transfers between devices with their start and end apart: 9, of which 5 were waited for; matrix products, arithmetic and copies ran while one was open for 1% of the time, Pallas kernels for 2%

profile of v6, /device:TPU:16, one launch (start us, length us, event | category | flops | bytes accessed | tf_op | source)
XLA Modules:
  0.0 44.4 jit_solution(13647043102032009531)
XLA Ops:
  0.0 6.1 %shard_map.91 = (f32[6,7,32,128]{3,2,1,0:T(8,128)S(1)}, f32[6,7,32,128]{3,2,1,0:T(8,128)S(1)}, f32[2,6,32,128]{3,2,1,0:T(8,128)S(1)}) custom-call(s32[1,6]{1,0:T(1,128)} %drift_hbm.1, bf16[1024,128]{1,0:T(8,128)(2,1)} %bitcast.339, f32[1024,128]{1,0:T(8,128)} %bitcast.338, bf16[512,512]{1,0:T(8,128)(2,1)} %constant.18.table_hbm, ...), custom_call_target="tpu_custom_call" | custom-call | flops 1000000000 | bytes 3145728 | tf_op jit(solution)/shard_map/pallas_call | solution.py:200
  6.1 0.1 collective-permute-start
  6.1 0.1 collective-permute-start.1
  6.3 2.0 %collective-permute-done = f32[6,7,32,128]{3,2,1,0:T(8,128)S(1)} collective-permute-done((f32[6,7,32,128]{3,2,1,0:T(8,128)S(1)}, f32[6,7,32,128]{3,2,1,0:T(8,128)S(1)}, u32[]{:S(2)}, u32[]{:S(2)}) %collective-permute-start) | collective-permute-done | bytes 688160 | tf_op jit(solution)/shard_map/ppermute | solution.py:302
  8.3 0.1 slice_subtract_fusion
  8.4 0.0 copy-start.2
  8.4 0.0 copy-start.1
  8.6 0.0 copy-start
  8.7 2.6 %collective-permute-start.2 = (f32[352,128]{1,0:T(8,128)S(1)}, f32[352,128]{1,0:T(8,128)S(1)}, u32[]{:S(2)}, u32[]{:S(2)}) collective-permute-start(f32[352,128]{1,0:T(8,128)S(1)} %bitcast.337), channel_id=1, source_target_pairs={{0,6},{1,7},{2,4},{3,5},{4,2},{5,3},{6,0},{7,1},{8,14},{9,15},{10,... | collective-permute-start | bytes 540680 | tf_op jit(solution)/shard_map/ppermute | solution.py:302
  11.3 0.5 %collective-permute-start.4 = (f32[352,128]{1,0:T(8,128)S(1)}, f32[352,128]{1,0:T(8,128)S(1)}, u32[]{:S(2)}, u32[]{:S(2)}) collective-permute-start(f32[352,128]{1,0:T(8,128)S(1)} %bitcast.336), channel_id=1, source_target_pairs={{0,2},{1,3},{2,0},{3,1},{4,6},{5,7},{6,4},{7,5},{8,10},{9,11},{10,... | collective-permute-start | bytes 540680 | tf_op jit(solution)/shard_map/ppermute | solution.py:302
  11.8 0.0 collective-permute-start.5
  11.8 3.8 %collective-permute-start.6 = (f32[352,128]{1,0:T(8,128)S(1)}, f32[352,128]{1,0:T(8,128)S(1)}, u32[]{:S(2)}, u32[]{:S(2)}) collective-permute-start(f32[352,128]{1,0:T(8,128)S(1)} %bitcast.334), channel_id=1, source_target_pairs={{0,10},{1,11},{2,8},{3,9},{4,14},{5,15},{6,12},{7,13},{8,2},{9,3},... | collective-permute-start | bytes 540680 | tf_op jit(solution)/shard_map/ppermute | solution.py:302
  15.5 0.2 collective-permute-done.1
  15.8 11.1 %collective-permute-start.7 = (f32[352,128]{1,0:T(8,128)S(1)}, f32[352,128]{1,0:T(8,128)S(1)}, u32[]{:S(2)}, u32[]{:S(2)}) collective-permute-start(f32[352,128]{1,0:T(8,128)S(1)} %bitcast.333), channel_id=1, source_target_pairs={{0,14},{1,15},{2,12},{3,13},{4,10},{5,11},{6,8},{7,9},{8,6},{9,7},... | collective-permute-start | bytes 540680 | tf_op jit(solution)/shard_map/ppermute | solution.py:302
  26.9 0.0 collective-permute-done.2.refs_3_
  26.9 1.0 %collective-permute-start.8 = (f32[352,128]{1,0:T(8,128)S(1)}, f32[352,128]{1,0:T(8,128)S(1)}, u32[]{:S(2)}, u32[]{:S(2)}) collective-permute-start(f32[352,128]{1,0:T(8,128)S(1)} %bitcast.332), channel_id=1, source_target_pairs={{0,4},{1,5},{2,6},{3,7},{4,0},{5,1},{6,2},{7,3},{8,12},{9,13},{10,... | collective-permute-start | bytes 540680 | tf_op jit(solution)/shard_map/ppermute | solution.py:302
  27.9 0.0 collective-permute-done.4.refs_3_
  27.9 0.1 collective-permute-start.3
  28.0 0.0 copy-done.2
  28.0 0.1 copy.13.tracks
  28.1 2.2 %collective-permute-done.5.refs_4_ = f32[352,128]{1,0:T(8,128)S(1)} collective-permute-done((f32[352,128]{1,0:T(8,128)S(1)}, f32[352,128]{1,0:T(8,128)S(1)}, u32[]{:S(2)}, u32[]{:S(2)}) %collective-permute-start.5) | collective-permute-done | bytes 180256 | tf_op jit(solution)/shard_map/ppermute | solution.py:302
  30.2 0.0 collective-permute-done.3
  30.3 0.0 copy-done.1
  30.3 1.0 %shard_map.92.refs_0_ = f32[64,4096]{1,0:T(8,128)S(1)} custom-call(s32[64,16]{1,0:T(8,128)S(1)} %copy.13.tracks, s32[3,45]{1,0:T(4,128)S(1)} %copy-done.1, f32[352,128]{1,0:T(8,128)S(1)} %bitcast.330, f32[192,128]{1,0:T(8,128)S(1)} %bitcast.329, f32[192,128]{1,0:T(8,128)S(1)} %bitcast.331, f32[352,128]{1,0:T(8,128)S(1)} %collective-permute-done.4.refs_3_, ...), custom_call_target="tpu_custom_call" | custom-call | tf_op jit(solution)/shard_map/pallas_call | solution.py:278
  31.2 3.9 %collective-permute-done.6.refs_1_ = f32[352,128]{1,0:T(8,128)S(1)} collective-permute-done((f32[352,128]{1,0:T(8,128)S(1)}, f32[352,128]{1,0:T(8,128)S(1)}, u32[]{:S(2)}, u32[]{:S(2)}) %collective-permute-start.6) | collective-permute-done | bytes 180256 | tf_op jit(solution)/shard_map/ppermute | solution.py:302
  35.1 7.7 %collective-permute-done.7.refs_2_ = f32[352,128]{1,0:T(8,128)S(1)} collective-permute-done((f32[352,128]{1,0:T(8,128)S(1)}, f32[352,128]{1,0:T(8,128)S(1)}, u32[]{:S(2)}, u32[]{:S(2)}) %collective-permute-start.7) | collective-permute-done | bytes 180256 | tf_op jit(solution)/shard_map/ppermute | solution.py:302
  42.8 0.0 collective-permute-done.8.refs_4_
  42.8 0.0 copy-done
  42.8 1.6 %shard_map.93 = f32[64,4096]{1,0:T(8,128)} custom-call(s32[64,16]{1,0:T(8,128)S(1)} %copy.13.tracks, s32[3,44]{1,0:T(4,128)S(1)} %copy-done, f32[64,4096]{1,0:T(8,128)S(1)} %shard_map.92.refs_0_, f32[352,128]{1,0:T(8,128)S(1)} %collective-permute-done.6.refs_1_, f32[352,128]{1,0:T(8,128)S(1)} %collective-permute-done.7.refs_2_, ...), custom_call_target="tpu_custom_call" | custom-call | tf_op jit(solution)/shard_map/pallas_call | solution.py:278
  (13 shorter events, 0.2 us)
Async XLA Ops:
  6.1 2.2 %collective-permute-start = (f32[6,7,32,128]{3,2,1,0:T(8,128)S(1)}, f32[6,7,32,128]{3,2,1,0:T(8,128)S(1)}, u32[]{:S(2)}, u32[]{:S(2)}) collective-permute-start(f32[6,7,32,128]{3,2,1,0:T(8,128)S(1)} %get-tuple-element.10), channel_id=1, source_target_pairs={{0,1},{1,0},{2,3},{3,2},{4,5},{5,4},{6,7},{7,6},{8,9},{9,8},{10,11... | collective-permute-start | bytes 2064392 | tf_op jit(solution)/shard_map/ppermute | solution.py:302
  6.1 9.6 %collective-permute-start.1 = (f32[2,6,32,128]{3,2,1,0:T(8,128)S(1)}, f32[2,6,32,128]{3,2,1,0:T(8,128)S(1)}, u32[]{:S(2)}, u32[]{:S(2)}) collective-permute-start(f32[2,6,32,128]{3,2,1,0:T(8,128)S(1)} %get-tuple-element.11), channel_id=1, source_target_pairs={{0,8},{1,9},{2,10},{3,11},{4,12},{5,13},{6,14},{7,15},{8,0},{9,1},... | collective-permute-start | bytes 589832 | tf_op jit(solution)/shard_map/ppermute | solution.py:302
  8.4 19.6 %copy-start.2 = (s32[64,16]{0,1:T(8,128)S(1)}, s32[64,16]{0,1:T(8,128)}, u32[]{:S(2)}) copy-start(s32[64,16]{0,1:T(8,128)} %param.12) | copy-start | bytes 12292
  8.4 21.8 %copy-start.1 = (s32[3,45]{1,0:T(4,128)S(1)}, s32[3,45]{1,0:T(4,128)}, u32[]{:S(2)}) copy-start(s32[3,45]{1,0:T(4,128)} %constant.13.clone.meta) | copy-start | bytes 1624
  8.6 34.2 %copy-start = (s32[3,44]{1,0:T(4,128)S(1)}, s32[3,44]{1,0:T(4,128)}, u32[]{:S(2)}) copy-start(s32[3,44]{1,0:T(4,128)} %constant.14.clone.meta) | copy-start | bytes 1588
  8.7 18.2 %collective-permute-start.2 = (f32[352,128]{1,0:T(8,128)S(1)}, f32[352,128]{1,0:T(8,128)S(1)}, u32[]{:S(2)}, u32[]{:S(2)}) collective-permute-start(f32[352,128]{1,0:T(8,128)S(1)} %bitcast.337), channel_id=1, source_target_pairs={{0,6},{1,7},{2,4},{3,5},{4,2},{5,3},{6,0},{7,1},{8,14},{9,15},{10,... | collective-permute-start | bytes 540680 | tf_op jit(solution)/shard_map/ppermute | solution.py:302
  11.3 16.6 %collective-permute-start.4 = (f32[352,128]{1,0:T(8,128)S(1)}, f32[352,128]{1,0:T(8,128)S(1)}, u32[]{:S(2)}, u32[]{:S(2)}) collective-permute-start(f32[352,128]{1,0:T(8,128)S(1)} %bitcast.336), channel_id=1, source_target_pairs={{0,2},{1,3},{2,0},{3,1},{4,6},{5,7},{6,4},{7,5},{8,10},{9,11},{10,... | collective-permute-start | bytes 540680 | tf_op jit(solution)/shard_map/ppermute | solution.py:302
  11.8 18.5 %collective-permute-start.5 = (f32[352,128]{1,0:T(8,128)S(1)}, f32[352,128]{1,0:T(8,128)S(1)}, u32[]{:S(2)}, u32[]{:S(2)}) collective-permute-start(f32[352,128]{1,0:T(8,128)S(1)} %bitcast.335), channel_id=1, source_target_pairs={{0,12},{1,13},{2,14},{3,15},{4,8},{5,9},{6,10},{7,11},{8,4},{9,5},... | collective-permute-start | bytes 540680 | tf_op jit(solution)/shard_map/ppermute | solution.py:302
  11.8 23.3 %collective-permute-start.6 = (f32[352,128]{1,0:T(8,128)S(1)}, f32[352,128]{1,0:T(8,128)S(1)}, u32[]{:S(2)}, u32[]{:S(2)}) collective-permute-start(f32[352,128]{1,0:T(8,128)S(1)} %bitcast.334), channel_id=1, source_target_pairs={{0,10},{1,11},{2,8},{3,9},{4,14},{5,15},{6,12},{7,13},{8,2},{9,3},... | collective-permute-start | bytes 540680 | tf_op jit(solution)/shard_map/ppermute | solution.py:302
  15.8 27.0 %collective-permute-start.7 = (f32[352,128]{1,0:T(8,128)S(1)}, f32[352,128]{1,0:T(8,128)S(1)}, u32[]{:S(2)}, u32[]{:S(2)}) collective-permute-start(f32[352,128]{1,0:T(8,128)S(1)} %bitcast.333), channel_id=1, source_target_pairs={{0,14},{1,15},{2,12},{3,13},{4,10},{5,11},{6,8},{7,9},{8,6},{9,7},... | collective-permute-start | bytes 540680 | tf_op jit(solution)/shard_map/ppermute | solution.py:302
  26.9 15.9 %collective-permute-start.8 = (f32[352,128]{1,0:T(8,128)S(1)}, f32[352,128]{1,0:T(8,128)S(1)}, u32[]{:S(2)}, u32[]{:S(2)}) collective-permute-start(f32[352,128]{1,0:T(8,128)S(1)} %bitcast.332), channel_id=1, source_target_pairs={{0,4},{1,5},{2,6},{3,7},{4,0},{5,1},{6,2},{7,3},{8,12},{9,13},{10,... | collective-permute-start | bytes 540680 | tf_op jit(solution)/shard_map/ppermute | solution.py:302
  27.9 2.4 %collective-permute-start.3 = (f32[6,32,128]{2,1,0:T(8,128)S(1)}, f32[6,32,128]{2,1,0:T(8,128)S(1)}, u32[]{:S(2)}, u32[]{:S(2)}) collective-permute-start(f32[6,32,128]{2,1,0:T(8,128)S(1)} %get-tuple-element.24), channel_id=1, source_target_pairs={{0,1},{1,0},{2,3},{3,2},{4,5},{5,4},{6,7},{7,6},{8,9},{9,8},{10,11... | collective-permute-start | bytes 294920 | tf_op jit(solution)/shard_map/ppermute | solution.py:302

commit v7 on v6

--- a/solution.py
+++ b/solution.py
@@ -37,10 +37,10 @@
 def chirp_table(rows, pairs):
     position = np.arange(rows * rows, dtype=np.float64) / (rows * rows)
     rates = (np.arange(KCOH) - (KCOH - 1) / 2.0) * CHIRP_STEP
-    rates = np.array([rates[KCOH - 1 - pair] for pair in pairs])
+    rates = rates[KCOH // 2 :][:1]
     angle = 2.0 * np.pi * rates[:, None] * (position * position)[None, :]
     table = np.stack([np.cos(angle), np.sin(angle)], 1)
-    return jnp.asarray(table.reshape(len(pairs), 2, rows, rows), F32)
+    return jnp.asarray(table.reshape(2, rows, rows), F32)
 
 
 def split_segment(weights, lanes, prep, coef):
@@ -122,7 +122,7 @@
         [
             (series_hbm, series),
             (weights_hbm, weights),
-            (chirp_hbm, chirp),
+            (chirp_hbm, chirp.at[KCOH // 2 - 1]),
             (table_hbm, table),
             (twist_hbm, twist),
             (drift_hbm, drift),
@@ -135,6 +135,12 @@
     split_segment(weights, lanes, prep, coef)
     for move in moves[2:]:
         move.wait()
+    last = KCOH // 2 - 1
+    cos, sin = chirp[last, 0], chirp[last, 1]
+    twice_cos, twice_sin = cos * cos - sin * sin, 2.0 * cos * sin
+    for at in reversed(range(last)):
+        cos, sin = cos * twice_cos - sin * twice_sin, sin * twice_cos + cos * twice_sin
+        chirp[at, 0], chirp[at, 1] = cos, sin
     per = own.shape[2]
     ones, spectra = {}, {}
 
@@ -295,7 +301,7 @@
     chips = count // 2
     half = chips // 2
     even_first = lambda away: (away % 2, away)
-    far, near = sorted(range(half, chips), key=even_first), list(range(1, half))
+    far, near = sorted(range(half, chips), key=even_first), sorted(range(1, half), key=even_first)
     order = [0] + far[:1] + near[:1] + far[1:] + near[:0:-1]
     early = order[: 1 + half - half // 4]
     swap = lambda hop: [(device, device ^ hop) for device in range(count)]

time: 44.9 us -> 44.6 us (level)
  starting transfers between devices: 19.2 us -> 11 us
  waiting for transfers between devices: 16 us -> 23.5 us
  local copies, waits for them, and re-layouts: 0.26 us -> 0.93 us
    ppermute x9, starting transfers between devices: 19.2 us -> 11 us  [local(): lax.ppermute(array, 'seg', swap(hop))]
    ppermute x9, waiting for transfers between devices: 16 us -> 23.5 us  [local(): lax.ppermute(array, 'seg', swap(hop))]
    unnamed x17, local copies, waits for them, and re-layouts: 0.24 us -> 0.91 us
  transfers between devices with their start and end apart: 9 -> 9, of which waited for: 5 -> 6; matrix products, arithmetic and copies ran while one was open for 1% -> 1% of each run, Pallas kernels for 2% -> 2%
where the time goes in v7:
time: 44.6 us; the launch traced here: 44.2 us
  waiting for transfers between devices  23.5 us (53%)
  starting transfers between devices  11 us (25%)
  Pallas kernels  8.42 us (19%)
  local copies, waits for them, and re-layouts  0.93 us (2%)
    ppermute x9, waiting for transfers between devices, local(): lax.ppermute(array, 'seg', swap(hop))  23.5 us
    ppermute x9, starting transfers between devices, local(): lax.ppermute(array, 'seg', swap(hop))  11 us
    pallas_call x1, Pallas kernels, stat(): pl.pallas_call(functools.partial(stat_kernel, kept, direct, count), out_s...  5.85 us
    pallas_call x2, Pallas kernels, track_sum(): pl.pallas_call(functools.partial(sum_kernel, plan, segments, len(starts))...  2.57 us
    unnamed x17, local copies, waits for them, and re-layouts  0.91 us
  transfers between devices with their start and end apart: 9, of which 6 were waited for; matrix products, arithmetic and copies ran while one was open for 1% of the time, Pallas kernels for 2%

profile of v7, /device:TPU:16, one launch (start us, length us, event | category | flops | bytes accessed | tf_op | source)
XLA Modules:
  0.0 44.2 jit_solution(9405315684859577624)
XLA Ops:
  0.0 5.8 %shard_map.91 = (f32[6,7,32,128]{3,2,1,0:T(8,128)S(1)}, f32[6,7,32,128]{3,2,1,0:T(8,128)S(1)}, f32[2,6,32,128]{3,2,1,0:T(8,128)S(1)}) custom-call(s32[1,6]{1,0:T(1,128)} %drift_hbm.1, bf16[1024,128]{1,0:T(8,128)(2,1)} %bitcast.339, f32[1024,128]{1,0:T(8,128)} %bitcast.338, bf16[512,512]{1,0:T(8,128)(2,1)} %constant.18.table_hbm, ...), custom_call_target="tpu_custom_call" | custom-call | flops 1000000000 | bytes 3145728 | tf_op jit(solution)/shard_map/pallas_call | solution.py:206
  5.9 0.1 collective-permute-start
  5.9 0.1 collective-permute-start.1
  6.0 2.0 %collective-permute-done = f32[6,7,32,128]{3,2,1,0:T(8,128)S(1)} collective-permute-done((f32[6,7,32,128]{3,2,1,0:T(8,128)S(1)}, f32[6,7,32,128]{3,2,1,0:T(8,128)S(1)}, u32[]{:S(2)}, u32[]{:S(2)}) %collective-permute-start) | collective-permute-done | bytes 688160 | tf_op jit(solution)/shard_map/ppermute | solution.py:308
  8.1 0.1 slice_subtract_fusion
  8.4 2.6 %collective-permute-start.2 = (f32[352,128]{1,0:T(8,128)S(1)}, f32[352,128]{1,0:T(8,128)S(1)}, u32[]{:S(2)}, u32[]{:S(2)}) collective-permute-start(f32[352,128]{1,0:T(8,128)S(1)} %bitcast.337), channel_id=1, source_target_pairs={{0,6},{1,7},{2,4},{3,5},{4,2},{5,3},{6,0},{7,1},{8,14},{9,15},{10,... | collective-permute-start | bytes 540680 | tf_op jit(solution)/shard_map/ppermute | solution.py:308
  11.0 0.4 %collective-permute-start.4 = (f32[352,128]{1,0:T(8,128)S(1)}, f32[352,128]{1,0:T(8,128)S(1)}, u32[]{:S(2)}, u32[]{:S(2)}) collective-permute-start(f32[352,128]{1,0:T(8,128)S(1)} %bitcast.336), channel_id=1, source_target_pairs={{0,4},{1,5},{2,6},{3,7},{4,0},{5,1},{6,2},{7,3},{8,12},{9,13},{10,... | collective-permute-start | bytes 540680 | tf_op jit(solution)/shard_map/ppermute | solution.py:308
  11.5 1.0 %collective-permute-start.5 = (f32[352,128]{1,0:T(8,128)S(1)}, f32[352,128]{1,0:T(8,128)S(1)}, u32[]{:S(2)}, u32[]{:S(2)}) collective-permute-start(f32[352,128]{1,0:T(8,128)S(1)} %bitcast.335), channel_id=1, source_target_pairs={{0,12},{1,13},{2,14},{3,15},{4,8},{5,9},{6,10},{7,11},{8,4},{9,5},... | collective-permute-start | bytes 540680 | tf_op jit(solution)/shard_map/ppermute | solution.py:308
  12.5 2.9 %collective-permute-start.6 = (f32[352,128]{1,0:T(8,128)S(1)}, f32[352,128]{1,0:T(8,128)S(1)}, u32[]{:S(2)}, u32[]{:S(2)}) collective-permute-start(f32[352,128]{1,0:T(8,128)S(1)} %bitcast.334), channel_id=1, source_target_pairs={{0,10},{1,11},{2,8},{3,9},{4,14},{5,15},{6,12},{7,13},{8,2},{9,3},... | collective-permute-start | bytes 540680 | tf_op jit(solution)/shard_map/ppermute | solution.py:308
  15.4 0.2 collective-permute-done.1
  15.6 3.4 %collective-permute-start.7 = (f32[352,128]{1,0:T(8,128)S(1)}, f32[352,128]{1,0:T(8,128)S(1)}, u32[]{:S(2)}, u32[]{:S(2)}) collective-permute-start(f32[352,128]{1,0:T(8,128)S(1)} %bitcast.333), channel_id=1, source_target_pairs={{0,14},{1,15},{2,12},{3,13},{4,10},{5,11},{6,8},{7,9},{8,6},{9,7},... | collective-permute-start | bytes 540680 | tf_op jit(solution)/shard_map/ppermute | solution.py:308
  19.0 1.1 %collective-permute-done.2.refs_3_ = f32[352,128]{1,0:T(8,128)S(1)} collective-permute-done((f32[352,128]{1,0:T(8,128)S(1)}, f32[352,128]{1,0:T(8,128)S(1)}, u32[]{:S(2)}, u32[]{:S(2)}) %collective-permute-start.2) | collective-permute-done | bytes 180256 | tf_op jit(solution)/shard_map/ppermute | solution.py:308
  20.1 0.0 copy-start.2
  20.1 0.5 %collective-permute-start.8 = (f32[352,128]{1,0:T(8,128)S(1)}, f32[352,128]{1,0:T(8,128)S(1)}, u32[]{:S(2)}, u32[]{:S(2)}) collective-permute-start(f32[352,128]{1,0:T(8,128)S(1)} %bitcast.332), channel_id=1, source_target_pairs={{0,2},{1,3},{2,0},{3,1},{4,6},{5,7},{6,4},{7,5},{8,10},{9,11},{10,... | collective-permute-start | bytes 540680 | tf_op jit(solution)/shard_map/ppermute | solution.py:308
  20.6 6.4 %collective-permute-done.4.refs_3_ = f32[352,128]{1,0:T(8,128)S(1)} collective-permute-done((f32[352,128]{1,0:T(8,128)S(1)}, f32[352,128]{1,0:T(8,128)S(1)}, u32[]{:S(2)}, u32[]{:S(2)}) %collective-permute-start.4) | collective-permute-done | bytes 180256 | tf_op jit(solution)/shard_map/ppermute | solution.py:308
  27.0 0.0 collective-permute-start.3
  27.0 0.0 copy-done.2
  27.0 0.1 copy.13.tracks
  27.1 6.8 %collective-permute-done.5.refs_4_ = f32[352,128]{1,0:T(8,128)S(1)} collective-permute-done((f32[352,128]{1,0:T(8,128)S(1)}, f32[352,128]{1,0:T(8,128)S(1)}, u32[]{:S(2)}, u32[]{:S(2)}) %collective-permute-start.5) | collective-permute-done | bytes 180256 | tf_op jit(solution)/shard_map/ppermute | solution.py:308
  33.9 0.0 collective-permute-done.3
  33.9 0.0 copy-start.1
  33.9 0.7 %copy-done.1 = s32[3,45]{1,0:T(4,128)S(1)} copy-done((s32[3,45]{1,0:T(4,128)S(1)}, s32[3,45]{1,0:T(4,128)}, u32[]{:S(2)}) %copy-start.1) | copy-done | bytes 564
  34.6 0.0 copy-start
  34.6 1.0 %shard_map.92.refs_0_ = f32[64,4096]{1,0:T(8,128)S(1)} custom-call(s32[64,16]{1,0:T(8,128)S(1)} %copy.13.tracks, s32[3,45]{1,0:T(4,128)S(1)} %copy-done.1, f32[352,128]{1,0:T(8,128)S(1)} %bitcast.330, f32[192,128]{1,0:T(8,128)S(1)} %bitcast.329, f32[192,128]{1,0:T(8,128)S(1)} %bitcast.331, f32[352,128]{1,0:T(8,128)S(1)} %collective-permute-done.4.refs_3_, ...), custom_call_target="tpu_custom_call" | custom-call | tf_op jit(solution)/shard_map/pallas_call | solution.py:284
  35.6 0.0 collective-permute-done.6.refs_1_
  35.6 7.0 %collective-permute-done.7.refs_2_ = f32[352,128]{1,0:T(8,128)S(1)} collective-permute-done((f32[352,128]{1,0:T(8,128)S(1)}, f32[352,128]{1,0:T(8,128)S(1)}, u32[]{:S(2)}, u32[]{:S(2)}) %collective-permute-start.7) | collective-permute-done | bytes 180256 | tf_op jit(solution)/shard_map/ppermute | solution.py:308
  42.5 0.0 collective-permute-done.8.refs_4_
  42.5 0.0 copy-done
  42.5 1.6 %shard_map.93 = f32[64,4096]{1,0:T(8,128)} custom-call(s32[64,16]{1,0:T(8,128)S(1)} %copy.13.tracks, s32[3,44]{1,0:T(4,128)S(1)} %copy-done, f32[64,4096]{1,0:T(8,128)S(1)} %shard_map.92.refs_0_, f32[352,128]{1,0:T(8,128)S(1)} %collective-permute-done.6.refs_1_, f32[352,128]{1,0:T(8,128)S(1)} %collective-permute-done.7.refs_2_, ...), custom_call_target="tpu_custom_call" | custom-call | tf_op jit(solution)/shard_map/pallas_call | solution.py:284
  (13 shorter events, 0.2 us)
Async XLA Ops:
  5.9 2.2 %collective-permute-start = (f32[6,7,32,128]{3,2,1,0:T(8,128)S(1)}, f32[6,7,32,128]{3,2,1,0:T(8,128)S(1)}, u32[]{:S(2)}, u32[]{:S(2)}) collective-permute-start(f32[6,7,32,128]{3,2,1,0:T(8,128)S(1)} %get-tuple-element.10), channel_id=1, source_target_pairs={{0,1},{1,0},{2,3},{3,2},{4,5},{5,4},{6,7},{7,6},{8,9},{9,8},{10,11... | collective-permute-start | bytes 2064392 | tf_op jit(solution)/shard_map/ppermute | solution.py:308
  5.9 9.6 %collective-permute-start.1 = (f32[2,6,32,128]{3,2,1,0:T(8,128)S(1)}, f32[2,6,32,128]{3,2,1,0:T(8,128)S(1)}, u32[]{:S(2)}, u32[]{:S(2)}) collective-permute-start(f32[2,6,32,128]{3,2,1,0:T(8,128)S(1)} %get-tuple-element.11), channel_id=1, source_target_pairs={{0,8},{1,9},{2,10},{3,11},{4,12},{5,13},{6,14},{7,15},{8,0},{9,1},... | collective-permute-start | bytes 589832 | tf_op jit(solution)/shard_map/ppermute | solution.py:308
  8.4 11.6 %collective-permute-start.2 = (f32[352,128]{1,0:T(8,128)S(1)}, f32[352,128]{1,0:T(8,128)S(1)}, u32[]{:S(2)}, u32[]{:S(2)}) collective-permute-start(f32[352,128]{1,0:T(8,128)S(1)} %bitcast.337), channel_id=1, source_target_pairs={{0,6},{1,7},{2,4},{3,5},{4,2},{5,3},{6,0},{7,1},{8,14},{9,15},{10,... | collective-permute-start | bytes 540680 | tf_op jit(solution)/shard_map/ppermute | solution.py:308
  11.0 15.9 %collective-permute-start.4 = (f32[352,128]{1,0:T(8,128)S(1)}, f32[352,128]{1,0:T(8,128)S(1)}, u32[]{:S(2)}, u32[]{:S(2)}) collective-permute-start(f32[352,128]{1,0:T(8,128)S(1)} %bitcast.336), channel_id=1, source_target_pairs={{0,4},{1,5},{2,6},{3,7},{4,0},{5,1},{6,2},{7,3},{8,12},{9,13},{10,... | collective-permute-start | bytes 540680 | tf_op jit(solution)/shard_map/ppermute | solution.py:308
  11.5 22.4 %collective-permute-start.5 = (f32[352,128]{1,0:T(8,128)S(1)}, f32[352,128]{1,0:T(8,128)S(1)}, u32[]{:S(2)}, u32[]{:S(2)}) collective-permute-start(f32[352,128]{1,0:T(8,128)S(1)} %bitcast.335), channel_id=1, source_target_pairs={{0,12},{1,13},{2,14},{3,15},{4,8},{5,9},{6,10},{7,11},{8,4},{9,5},... | collective-permute-start | bytes 540680 | tf_op jit(solution)/shard_map/ppermute | solution.py:308
  12.5 23.1 %collective-permute-start.6 = (f32[352,128]{1,0:T(8,128)S(1)}, f32[352,128]{1,0:T(8,128)S(1)}, u32[]{:S(2)}, u32[]{:S(2)}) collective-permute-start(f32[352,128]{1,0:T(8,128)S(1)} %bitcast.334), channel_id=1, source_target_pairs={{0,10},{1,11},{2,8},{3,9},{4,14},{5,15},{6,12},{7,13},{8,2},{9,3},... | collective-permute-start | bytes 540680 | tf_op jit(solution)/shard_map/ppermute | solution.py:308
  15.6 27.0 %collective-permute-start.7 = (f32[352,128]{1,0:T(8,128)S(1)}, f32[352,128]{1,0:T(8,128)S(1)}, u32[]{:S(2)}, u32[]{:S(2)}) collective-permute-start(f32[352,128]{1,0:T(8,128)S(1)} %bitcast.333), channel_id=1, source_target_pairs={{0,14},{1,15},{2,12},{3,13},{4,10},{5,11},{6,8},{7,9},{8,6},{9,7},... | collective-permute-start | bytes 540680 | tf_op jit(solution)/shard_map/ppermute | solution.py:308
  20.1 6.9 %copy-start.2 = (s32[64,16]{0,1:T(8,128)S(1)}, s32[64,16]{0,1:T(8,128)}, u32[]{:S(2)}) copy-start(s32[64,16]{0,1:T(8,128)} %param.12) | copy-start | bytes 12292
  20.1 22.5 %collective-permute-start.8 = (f32[352,128]{1,0:T(8,128)S(1)}, f32[352,128]{1,0:T(8,128)S(1)}, u32[]{:S(2)}, u32[]{:S(2)}) collective-permute-start(f32[352,128]{1,0:T(8,128)S(1)} %bitcast.332), channel_id=1, source_target_pairs={{0,2},{1,3},{2,0},{3,1},{4,6},{5,7},{6,4},{7,5},{8,10},{9,11},{10,... | collective-permute-start | bytes 540680 | tf_op jit(solution)/shard_map/ppermute | solution.py:308
  27.0 6.9 %collective-permute-start.3 = (f32[6,32,128]{2,1,0:T(8,128)S(1)}, f32[6,32,128]{2,1,0:T(8,128)S(1)}, u32[]{:S(2)}, u32[]{:S(2)}) collective-permute-start(f32[6,32,128]{2,1,0:T(8,128)S(1)} %get-tuple-element.24), channel_id=1, source_target_pairs={{0,1},{1,0},{2,3},{3,2},{4,5},{5,4},{6,7},{7,6},{8,9},{9,8},{10,11... | collective-permute-start | bytes 294920 | tf_op jit(solution)/shard_map/ppermute | solution.py:308
  33.9 0.7 %copy-start.1 = (s32[3,45]{1,0:T(4,128)S(1)}, s32[3,45]{1,0:T(4,128)}, u32[]{:S(2)}) copy-start(s32[3,45]{1,0:T(4,128)} %constant.13.clone.meta) | copy-start | bytes 1624
  34.6 8.0 %copy-start = (s32[3,44]{1,0:T(4,128)S(1)}, s32[3,44]{1,0:T(4,128)}, u32[]{:S(2)}) copy-start(s32[3,44]{1,0:T(4,128)} %constant.14.clone.meta) | copy-start | bytes 1588

commit v8 on v7

--- a/solution.py
+++ b/solution.py
@@ -304,6 +304,7 @@
     far, near = sorted(range(half, chips), key=even_first), sorted(range(1, half), key=even_first)
     order = [0] + far[:1] + near[:1] + far[1:] + near[:0:-1]
     early = order[: 1 + half - half // 4]
+    early += [away for away in near[-1:] if away not in early]
     swap = lambda hop: [(device, device ^ hop) for device in range(count)]
     send = lambda array, hop: lax.ppermute(array, "seg", swap(hop)) if hop else array
     pack = lambda rows: jnp.stack(rows).reshape(-1, BLK)

time: 44.6 us -> 44.4 us (level)
  no operation moved by 1% of the time
where the time goes in v8:
time: 44.4 us; the launch traced here: 44 us
  waiting for transfers between devices  23.4 us (53%)
  starting transfers between devices  11 us (25%)
  Pallas kernels  8.37 us (19%)
  local copies, waits for them, and re-layouts  0.93 us (2%)
    ppermute x9, waiting for transfers between devices, local(): lax.ppermute(array, 'seg', swap(hop))  23.4 us
    ppermute x9, starting transfers between devices, local(): lax.ppermute(array, 'seg', swap(hop))  11 us
    pallas_call x1, Pallas kernels, stat(): pl.pallas_call(functools.partial(stat_kernel, kept, direct, count), out_s...  5.85 us
    pallas_call x2, Pallas kernels, track_sum(): pl.pallas_call(functools.partial(sum_kernel, plan, segments, len(starts))...  2.52 us
    unnamed x17, local copies, waits for them, and re-layouts  0.91 us
  transfers between devices with their start and end apart: 9, of which 6 were waited for; matrix products, arithmetic and copies ran while one was open for 1% of the time, Pallas kernels for 2%

profile of v8, /device:TPU:16, one launch (start us, length us, event | category | flops | bytes accessed | tf_op | source)
XLA Modules:
  0.0 44.0 jit_solution(11306909773111910642)
XLA Ops:
  0.0 5.8 %shard_map.91 = (f32[6,7,32,128]{3,2,1,0:T(8,128)S(1)}, f32[6,7,32,128]{3,2,1,0:T(8,128)S(1)}, f32[2,6,32,128]{3,2,1,0:T(8,128)S(1)}) custom-call(s32[1,6]{1,0:T(1,128)} %drift_hbm.1, bf16[1024,128]{1,0:T(8,128)(2,1)} %bitcast.339, f32[1024,128]{1,0:T(8,128)} %bitcast.338, bf16[512,512]{1,0:T(8,128)(2,1)} %constant.18.table_hbm, ...), custom_call_target="tpu_custom_call" | custom-call | flops 1000000000 | bytes 3145728 | tf_op jit(solution)/shard_map/pallas_call | solution.py:206
  5.9 0.1 collective-permute-start
  5.9 0.1 collective-permute-start.1
  6.0 2.0 %collective-permute-done = f32[6,7,32,128]{3,2,1,0:T(8,128)S(1)} collective-permute-done((f32[6,7,32,128]{3,2,1,0:T(8,128)S(1)}, f32[6,7,32,128]{3,2,1,0:T(8,128)S(1)}, u32[]{:S(2)}, u32[]{:S(2)}) %collective-permute-start) | collective-permute-done | bytes 688160 | tf_op jit(solution)/shard_map/ppermute | solution.py:309
  8.1 0.1 slice_subtract_fusion
  8.4 2.6 %collective-permute-start.2 = (f32[352,128]{1,0:T(8,128)S(1)}, f32[352,128]{1,0:T(8,128)S(1)}, u32[]{:S(2)}, u32[]{:S(2)}) collective-permute-start(f32[352,128]{1,0:T(8,128)S(1)} %bitcast.337), channel_id=1, source_target_pairs={{0,6},{1,7},{2,4},{3,5},{4,2},{5,3},{6,0},{7,1},{8,14},{9,15},{10,... | collective-permute-start | bytes 540680 | tf_op jit(solution)/shard_map/ppermute | solution.py:309
  11.0 0.4 %collective-permute-start.4 = (f32[352,128]{1,0:T(8,128)S(1)}, f32[352,128]{1,0:T(8,128)S(1)}, u32[]{:S(2)}, u32[]{:S(2)}) collective-permute-start(f32[352,128]{1,0:T(8,128)S(1)} %bitcast.336), channel_id=1, source_target_pairs={{0,4},{1,5},{2,6},{3,7},{4,0},{5,1},{6,2},{7,3},{8,12},{9,13},{10,... | collective-permute-start | bytes 540680 | tf_op jit(solution)/shard_map/ppermute | solution.py:309
  11.5 1.0 %collective-permute-start.5 = (f32[352,128]{1,0:T(8,128)S(1)}, f32[352,128]{1,0:T(8,128)S(1)}, u32[]{:S(2)}, u32[]{:S(2)}) collective-permute-start(f32[352,128]{1,0:T(8,128)S(1)} %bitcast.335), channel_id=1, source_target_pairs={{0,12},{1,13},{2,14},{3,15},{4,8},{5,9},{6,10},{7,11},{8,4},{9,5},... | collective-permute-start | bytes 540680 | tf_op jit(solution)/shard_map/ppermute | solution.py:309
  12.5 2.9 %collective-permute-start.6 = (f32[352,128]{1,0:T(8,128)S(1)}, f32[352,128]{1,0:T(8,128)S(1)}, u32[]{:S(2)}, u32[]{:S(2)}) collective-permute-start(f32[352,128]{1,0:T(8,128)S(1)} %bitcast.334), channel_id=1, source_target_pairs={{0,10},{1,11},{2,8},{3,9},{4,14},{5,15},{6,12},{7,13},{8,2},{9,3},... | collective-permute-start | bytes 540680 | tf_op jit(solution)/shard_map/ppermute | solution.py:309
  15.4 0.2 collective-permute-done.1
  15.6 3.4 %collective-permute-start.7 = (f32[352,128]{1,0:T(8,128)S(1)}, f32[352,128]{1,0:T(8,128)S(1)}, u32[]{:S(2)}, u32[]{:S(2)}) collective-permute-start(f32[352,128]{1,0:T(8,128)S(1)} %bitcast.333), channel_id=1, source_target_pairs={{0,14},{1,15},{2,12},{3,13},{4,10},{5,11},{6,8},{7,9},{8,6},{9,7},... | collective-permute-start | bytes 540680 | tf_op jit(solution)/shard_map/ppermute | solution.py:309
  19.0 1.1 %collective-permute-done.2.refs_5_ = f32[352,128]{1,0:T(8,128)S(1)} collective-permute-done((f32[352,128]{1,0:T(8,128)S(1)}, f32[352,128]{1,0:T(8,128)S(1)}, u32[]{:S(2)}, u32[]{:S(2)}) %collective-permute-start.2) | collective-permute-done | bytes 180256 | tf_op jit(solution)/shard_map/ppermute | solution.py:309
  20.1 0.0 copy-start.2
  20.1 0.5 %collective-permute-start.8 = (f32[352,128]{1,0:T(8,128)S(1)}, f32[352,128]{1,0:T(8,128)S(1)}, u32[]{:S(2)}, u32[]{:S(2)}) collective-permute-start(f32[352,128]{1,0:T(8,128)S(1)} %bitcast.332), channel_id=1, source_target_pairs={{0,2},{1,3},{2,0},{3,1},{4,6},{5,7},{6,4},{7,5},{8,10},{9,11},{10,... | collective-permute-start | bytes 540680 | tf_op jit(solution)/shard_map/ppermute | solution.py:309
  20.6 6.4 %collective-permute-done.4.refs_3_ = f32[352,128]{1,0:T(8,128)S(1)} collective-permute-done((f32[352,128]{1,0:T(8,128)S(1)}, f32[352,128]{1,0:T(8,128)S(1)}, u32[]{:S(2)}, u32[]{:S(2)}) %collective-permute-start.4) | collective-permute-done | bytes 180256 | tf_op jit(solution)/shard_map/ppermute | solution.py:309
  27.0 0.0 collective-permute-start.3
  27.0 0.0 copy-done.2
  27.0 0.1 copy.13.tracks
  27.1 6.8 %collective-permute-done.5.refs_4_ = f32[352,128]{1,0:T(8,128)S(1)} collective-permute-done((f32[352,128]{1,0:T(8,128)S(1)}, f32[352,128]{1,0:T(8,128)S(1)}, u32[]{:S(2)}, u32[]{:S(2)}) %collective-permute-start.5) | collective-permute-done | bytes 180256 | tf_op jit(solution)/shard_map/ppermute | solution.py:309
  33.9 0.0 collective-permute-done.3
  33.9 0.0 copy-start.1
  33.9 0.7 %copy-done.1 = s32[3,56]{1,0:T(4,128)S(1)} copy-done((s32[3,56]{1,0:T(4,128)S(1)}, s32[3,56]{1,0:T(4,128)}, u32[]{:S(2)}) %copy-start.1) | copy-done | bytes 696
  34.6 0.0 copy-start
  34.6 1.1 %shard_map.92.refs_0_ = f32[64,4096]{1,0:T(8,128)S(1)} custom-call(s32[64,16]{1,0:T(8,128)S(1)} %copy.13.tracks, s32[3,56]{1,0:T(4,128)S(1)} %copy-done.1, f32[352,128]{1,0:T(8,128)S(1)} %bitcast.330, f32[192,128]{1,0:T(8,128)S(1)} %bitcast.329, f32[192,128]{1,0:T(8,128)S(1)} %bitcast.331, f32[352,128]{1,0:T(8,128)S(1)} %collective-permute-done.4.refs_3_, ...), custom_call_target="tpu_custom_call" | custom-call | tf_op jit(solution)/shard_map/pallas_call | solution.py:284
  35.7 0.0 collective-permute-done.6.refs_1_
  35.7 6.8 %collective-permute-done.7.refs_2_ = f32[352,128]{1,0:T(8,128)S(1)} collective-permute-done((f32[352,128]{1,0:T(8,128)S(1)}, f32[352,128]{1,0:T(8,128)S(1)}, u32[]{:S(2)}, u32[]{:S(2)}) %collective-permute-start.7) | collective-permute-done | bytes 180256 | tf_op jit(solution)/shard_map/ppermute | solution.py:309
  42.5 0.0 collective-permute-done.8.refs_3_
  42.5 0.0 copy-done
  42.5 1.4 %shard_map.93 = f32[64,4096]{1,0:T(8,128)} custom-call(s32[64,16]{1,0:T(8,128)S(1)} %copy.13.tracks, s32[3,33]{1,0:T(4,128)S(1)} %copy-done, f32[64,4096]{1,0:T(8,128)S(1)} %shard_map.92.refs_0_, f32[352,128]{1,0:T(8,128)S(1)} %collective-permute-done.6.refs_1_, f32[352,128]{1,0:T(8,128)S(1)} %collective-permute-done.7.refs_2_, ...), custom_call_target="tpu_custom_call" | custom-call | tf_op jit(solution)/shard_map/pallas_call | solution.py:284
  (13 shorter events, 0.2 us)
Async XLA Ops:
  5.9 2.2 %collective-permute-start = (f32[6,7,32,128]{3,2,1,0:T(8,128)S(1)}, f32[6,7,32,128]{3,2,1,0:T(8,128)S(1)}, u32[]{:S(2)}, u32[]{:S(2)}) collective-permute-start(f32[6,7,32,128]{3,2,1,0:T(8,128)S(1)} %get-tuple-element.10), channel_id=1, source_target_pairs={{0,1},{1,0},{2,3},{3,2},{4,5},{5,4},{6,7},{7,6},{8,9},{9,8},{10,11... | collective-permute-start | bytes 2064392 | tf_op jit(solution)/shard_map/ppermute | solution.py:309
  5.9 9.6 %collective-permute-start.1 = (f32[2,6,32,128]{3,2,1,0:T(8,128)S(1)}, f32[2,6,32,128]{3,2,1,0:T(8,128)S(1)}, u32[]{:S(2)}, u32[]{:S(2)}) collective-permute-start(f32[2,6,32,128]{3,2,1,0:T(8,128)S(1)} %get-tuple-element.11), channel_id=1, source_target_pairs={{0,8},{1,9},{2,10},{3,11},{4,12},{5,13},{6,14},{7,15},{8,0},{9,1},... | collective-permute-start | bytes 589832 | tf_op jit(solution)/shard_map/ppermute | solution.py:309
  8.4 11.6 %collective-permute-start.2 = (f32[352,128]{1,0:T(8,128)S(1)}, f32[352,128]{1,0:T(8,128)S(1)}, u32[]{:S(2)}, u32[]{:S(2)}) collective-permute-start(f32[352,128]{1,0:T(8,128)S(1)} %bitcast.337), channel_id=1, source_target_pairs={{0,6},{1,7},{2,4},{3,5},{4,2},{5,3},{6,0},{7,1},{8,14},{9,15},{10,... | collective-permute-start | bytes 540680 | tf_op jit(solution)/shard_map/ppermute | solution.py:309
  11.0 15.9 %collective-permute-start.4 = (f32[352,128]{1,0:T(8,128)S(1)}, f32[352,128]{1,0:T(8,128)S(1)}, u32[]{:S(2)}, u32[]{:S(2)}) collective-permute-start(f32[352,128]{1,0:T(8,128)S(1)} %bitcast.336), channel_id=1, source_target_pairs={{0,4},{1,5},{2,6},{3,7},{4,0},{5,1},{6,2},{7,3},{8,12},{9,13},{10,... | collective-permute-start | bytes 540680 | tf_op jit(solution)/shard_map/ppermute | solution.py:309
  11.5 22.4 %collective-permute-start.5 = (f32[352,128]{1,0:T(8,128)S(1)}, f32[352,128]{1,0:T(8,128)S(1)}, u32[]{:S(2)}, u32[]{:S(2)}) collective-permute-start(f32[352,128]{1,0:T(8,128)S(1)} %bitcast.335), channel_id=1, source_target_pairs={{0,12},{1,13},{2,14},{3,15},{4,8},{5,9},{6,10},{7,11},{8,4},{9,5},... | collective-permute-start | bytes 540680 | tf_op jit(solution)/shard_map/ppermute | solution.py:309
  12.5 23.2 %collective-permute-start.6 = (f32[352,128]{1,0:T(8,128)S(1)}, f32[352,128]{1,0:T(8,128)S(1)}, u32[]{:S(2)}, u32[]{:S(2)}) collective-permute-start(f32[352,128]{1,0:T(8,128)S(1)} %bitcast.334), channel_id=1, source_target_pairs={{0,10},{1,11},{2,8},{3,9},{4,14},{5,15},{6,12},{7,13},{8,2},{9,3},... | collective-permute-start | bytes 540680 | tf_op jit(solution)/shard_map/ppermute | solution.py:309
  15.6 27.0 %collective-permute-start.7 = (f32[352,128]{1,0:T(8,128)S(1)}, f32[352,128]{1,0:T(8,128)S(1)}, u32[]{:S(2)}, u32[]{:S(2)}) collective-permute-start(f32[352,128]{1,0:T(8,128)S(1)} %bitcast.333), channel_id=1, source_target_pairs={{0,14},{1,15},{2,12},{3,13},{4,10},{5,11},{6,8},{7,9},{8,6},{9,7},... | collective-permute-start | bytes 540680 | tf_op jit(solution)/shard_map/ppermute | solution.py:309
  20.1 6.9 %copy-start.2 = (s32[64,16]{0,1:T(8,128)S(1)}, s32[64,16]{0,1:T(8,128)}, u32[]{:S(2)}) copy-start(s32[64,16]{0,1:T(8,128)} %param.12) | copy-start | bytes 12292
  20.1 22.5 %collective-permute-start.8 = (f32[352,128]{1,0:T(8,128)S(1)}, f32[352,128]{1,0:T(8,128)S(1)}, u32[]{:S(2)}, u32[]{:S(2)}) collective-permute-start(f32[352,128]{1,0:T(8,128)S(1)} %bitcast.332), channel_id=1, source_target_pairs={{0,2},{1,3},{2,0},{3,1},{4,6},{5,7},{6,4},{7,5},{8,10},{9,11},{10,... | collective-permute-start | bytes 540680 | tf_op jit(solution)/shard_map/ppermute | solution.py:309
  27.0 6.9 %collective-permute-start.3 = (f32[6,32,128]{2,1,0:T(8,128)S(1)}, f32[6,32,128]{2,1,0:T(8,128)S(1)}, u32[]{:S(2)}, u32[]{:S(2)}) collective-permute-start(f32[6,32,128]{2,1,0:T(8,128)S(1)} %get-tuple-element.24), channel_id=1, source_target_pairs={{0,1},{1,0},{2,3},{3,2},{4,5},{5,4},{6,7},{7,6},{8,9},{9,8},{10,11... | collective-permute-start | bytes 294920 | tf_op jit(solution)/shard_map/ppermute | solution.py:309
  33.9 0.7 %copy-start.1 = (s32[3,56]{1,0:T(4,128)S(1)}, s32[3,56]{1,0:T(4,128)}, u32[]{:S(2)}) copy-start(s32[3,56]{1,0:T(4,128)} %constant.13.clone.meta) | copy-start | bytes 2020
  34.6 8.0 %copy-start = (s32[3,33]{1,0:T(4,128)S(1)}, s32[3,33]{1,0:T(4,128)}, u32[]{:S(2)}) copy-start(s32[3,33]{1,0:T(4,128)} %constant.14.clone.meta) | copy-start | bytes 1192
